TPU v7x, 128 devices: a whole 4x4x4 slice. The times are simulated.
128 devices in a mesh: row: 8 (over z, x_hi), col: 8 (over y, core), tm: 2 (over x_lo).
Axes of the slice: x: 4 (x_hi: 2, x_lo: 2; x = x_hi * 2 + x_lo), y: 4, z: 4, core: 2. Of those that a mesh axis runs over, the one named last changes fastest.
Arguments:
- tile_values: bfloat16 [8, 8, 2, 384, 128, 128], P('row', 'col', 'tm'), may hold values from -6 to 6
- tile_coords: int32 [8, 8, 2, 3, 384], P('row', 'col', 'tm'), may hold values from 0 to 31, as said below
- tile_counts: int32 [8, 8, 2], P('row', 'col', 'tm'), may hold values from 96 to 384, as said below
- factor_rows: bfloat16 [8, 2048, 256], P('row', ('col', 'tm')), may hold values from -0.23925781 to 0.23925781
- factor_cols: bfloat16 [8, 2048, 256], P('col', ('row', 'tm')), may hold values from -0.23925781 to 0.23925781
- factor_time: bfloat16 [64, 256], P('tm'), may hold values from -0.76953125 to 0.76953125
Outputs:
- grad_rows: float32 [8, 2048, 256], P('row', ('col', 'tm'))
- grad_cols: float32 [8, 2048, 256], P('col', ('row', 'tm'))
- grad_time: float32 [64, 256], P('tm')
Inputs may be any that keep to these rules, and one draw needn't show every extreme that they name: `tile_coords`: on each device the 384 slots name distinct triples; row block below 16, column block below 16, snapshot below 32. Only the first tile_counts slots of a device are live; some device has all 384 live in every draw.
All inputs are finite; a program needn't handle non-finite values.
Results may differ from a plain program's by a relative error of at most 0.0003.
Values may be sent and summed in bfloat16 or wider, within the bound.
A program may use at most 128 MiB of HBM per device.

v0:
```python
import math

import jax
import jax.numpy as jnp
from jax import lax
from jax.sharding import PartitionSpec as P


def on_device(tile_values, tile_coords, tile_counts, factor_rows, factor_cols, factor_time):
    tile_vals = tile_values[0, 0, 0]
    places = tile_coords[0, 0, 0]
    live_count = tile_counts[0, 0, 0]
    slot_count = tile_vals.shape[0]
    tile_edge = tile_vals.shape[1]
    rank_width = factor_rows.shape[2]
    highest = lax.Precision.HIGHEST
    live_slots = jnp.arange(slot_count, dtype=jnp.int32) < live_count
    tile_vals = jnp.where(live_slots[:, None, None], tile_vals, jnp.zeros((), tile_vals.dtype))
    row_block = lax.all_gather(factor_rows, ("col", "tm"), axis=1, tiled=True)
    col_block = lax.all_gather(factor_cols, ("row", "tm"), axis=1, tiled=True)
    row_flat = row_block[0].reshape(-1, tile_edge * rank_width)
    col_flat = col_block[0].reshape(-1, tile_edge * rank_width)
    row_count = row_flat.shape[0]
    col_count = col_flat.shape[0]
    time_whole = lax.all_gather(factor_time, "tm", axis=0, tiled=True)
    section = factor_time.shape[0]
    block_size = math.gcd(slot_count, 64)
    block_count = slot_count // block_size
    row_ids = jnp.arange(row_count, dtype=jnp.int32)
    col_ids = jnp.arange(col_count, dtype=jnp.int32)
    time_ids = jnp.arange(section, dtype=jnp.int32)

    def add_block(totals, inputs):
        sum_rows, sum_cols, sum_time = totals
        block_vals, block_place = inputs
        row_hot = (block_place[0][:, None] == row_ids[None, :]).astype(jnp.bfloat16)
        col_hot = (block_place[1][:, None] == col_ids[None, :]).astype(jnp.bfloat16)
        time_hot = (block_place[2][:, None] == time_ids[None, :]).astype(jnp.bfloat16)
        row_take = (
            jnp.dot(row_hot, row_flat, preferred_element_type=jnp.float32)
            .astype(jnp.bfloat16)
            .reshape(block_size, tile_edge, rank_width)
        )
        col_take = (
            jnp.dot(col_hot, col_flat, preferred_element_type=jnp.float32)
            .astype(jnp.bfloat16)
            .reshape(block_size, tile_edge, rank_width)
        )
        time_take = jnp.dot(time_hot, factor_time, preferred_element_type=jnp.float32)
        prod_cols = jnp.einsum(
            "nij,njr->nir", block_vals, col_take, preferred_element_type=jnp.float32
        )
        prod_rows = jnp.einsum(
            "nij,nir->njr", block_vals, row_take, preferred_element_type=jnp.float32
        )
        row_terms = (prod_cols * time_take[:, None, :]).reshape(block_size, -1)
        col_terms = (prod_rows * time_take[:, None, :]).reshape(block_size, -1)
        time_terms = jnp.sum(row_take.astype(jnp.float32) * prod_cols, axis=1)
        sum_rows = sum_rows + jnp.einsum(
            "na,nx->ax", row_hot.astype(jnp.float32), row_terms, precision=highest
        )
        sum_cols = sum_cols + jnp.einsum(
            "na,nx->ax", col_hot.astype(jnp.float32), col_terms, precision=highest
        )
        sum_time = sum_time + jnp.einsum(
            "nk,nr->kr", time_hot.astype(jnp.float32), time_terms, precision=highest
        )
        return ((sum_rows, sum_cols, sum_time), None)

    init_sums = (
        jnp.zeros(row_flat.shape, jnp.float32),
        jnp.zeros(col_flat.shape, jnp.float32),
        jnp.zeros((section, rank_width), jnp.float32),
    )
    block_inputs = (
        tile_vals.reshape(block_count, block_size, tile_edge, tile_edge),
        jnp.transpose(places.reshape(3, block_count, block_size), (1, 0, 2)),
    )
    (sum_rows, sum_cols, sum_time), unused = lax.scan(add_block, init_sums, block_inputs)
    sum_rows = sum_rows.reshape(1, -1, rank_width)
    sum_cols = sum_cols.reshape(1, -1, rank_width)
    mttkrp_rows = lax.psum_scatter(sum_rows, ("col", "tm"), scatter_dimension=1, tiled=True)
    mttkrp_cols = lax.psum_scatter(sum_cols, ("row", "tm"), scatter_dimension=1, tiled=True)
    own_rows = factor_rows[0]
    own_cols = factor_cols[0]
    gram_rows_part = jnp.einsum("ir,is->rs", own_rows, own_rows, preferred_element_type=jnp.float32)
    gram_cols_part = jnp.einsum("ir,is->rs", own_cols, own_cols, preferred_element_type=jnp.float32)
    gram_time = jnp.einsum("ir,is->rs", time_whole, time_whole, preferred_element_type=jnp.float32)
    gram_rows, gram_cols = lax.psum((gram_rows_part, gram_cols_part), ("row", "col", "tm"))
    mttkrp_time = lax.psum(sum_time, ("row", "col"))
    grad_rows = (
        jnp.dot(own_rows.astype(jnp.float32), gram_cols * gram_time, precision=highest)
        - mttkrp_rows[0]
    )
    grad_cols = (
        jnp.dot(own_cols.astype(jnp.float32), gram_rows * gram_time, precision=highest)
        - mttkrp_cols[0]
    )
    grad_time = (
        jnp.dot(factor_time.astype(jnp.float32), gram_rows * gram_cols, precision=highest)
        - mttkrp_time
    )
    return (grad_rows[None], grad_cols[None], grad_time)


def solution(mesh):
    return jax.shard_map(
        on_device,
        mesh=mesh,
        in_specs=(
            P("row", "col", "tm", None, None, None),
            P("row", "col", "tm", None, None),
            P("row", "col", "tm"),
            P("row", ("col", "tm"), None),
            P("col", ("row", "tm"), None),
            P("tm", None),
        ),
        out_specs=(P("row", ("col", "tm"), None), P("col", ("row", "tm"), None), P("tm", None)),
        check_vma=False,
    )
```

profile of v0, /device:TPU:0, one launch (start us, length us, event | category | flops | bytes accessed | tf_op | source)
XLA Modules:
  0.0 679.0 jit_solution(12419626052311615030)
XLA Ops:
  14.7 10.6 %broadcast_select_fusion = bf16[6,64,128,128]{3,2,1,0:T(8,128)(2,1)} fusion(bf16[6,64,128,128]{3,2,1,0:T(8,128)(2,1)} %bitcast.125, pred[6,64]{1,0:T(8,128)(4,1)S(1)} %add_compare_fusion), kind=kLoop, calls=%fused_computation.33 | loop fusion | flops 6291456 | bytes 25166208 | tf_op jit(solution)/shard_map/jit(_where)/select_n | solution.py:18
  25.3 31.3 %all-gather.3.cloned.1.call-done = bf16[1,2048,256]{2,1,0:T(8,128)(2,1)} async-done(((bf16[1,128,256]{2,1,0:T(8,128)(2,1)}), bf16[1,2048,256]{2,1,0:T(8,128)(2,1)}) %all-gather.3.cloned.1.call-update) | async-done | bytes 1048592 | tf_op jit(solution)/shard_map/all_gather | solution.py:20
  58.2 45.2 %all-gather.5.cloned.1.call-done = bf16[1,2048,256]{2,1,0:T(8,128)(2,1)} async-done(((bf16[1,128,256]{2,1,0:T(8,128)(2,1)}), bf16[1,2048,256]{2,1,0:T(8,128)(2,1)}) %all-gather.5.cloned.1.call-update) | async-done | bytes 1048592 | tf_op jit(solution)/shard_map/all_gather | solution.py:19
  105.7 216.8 %while.17 = (s32[]{:T(128)}, f32[16,32768]{1,0:T(8,128)S(1)}, f32[16,32768]{1,0:T(8,128)}, f32[32,256]{1,0:T(8,128)S(1)}, s32[6,3,64]{2,0,1:T(8,128)S(1)}, /*ind...) while((s32[]{:T(128)}, f32[16,32768]{1,0:T(8,128)S(1)}, ...), condition=%wide.region_3.4_spmd.clone.clone, body=%wide.region_1.3_spmd.clone.clone.sunk | while | flops 2037391360 | bytes 153506032 | solution.py:79
  115.2 7.9 %copy.33 = f32[8,8,128,256]{3,1,2,0:T(8,128)} copy(f32[8,8,128,256]{3,2,1,0:T(8,128)S(1)} %bitcast.120) | data formatting | bytes 16777216 | tf_op jit(solution)/shard_map/while
  123.1 5.6 convolution_add_fusion.6
  132.0 4.7 copy.34
  150.3 7.9 %copy.33 = f32[8,8,128,256]{3,1,2,0:T(8,128)} copy(f32[8,8,128,256]{3,2,1,0:T(8,128)S(1)} %bitcast.120) | data formatting | bytes 16777216 | tf_op jit(solution)/shard_map/while
  158.3 5.6 convolution_add_fusion.6
  167.1 4.7 copy.34
  171.9 5.3 convolution_add_fusion.7
  186.6 7.9 %copy.33 = f32[8,8,128,256]{3,1,2,0:T(8,128)} copy(f32[8,8,128,256]{3,2,1,0:T(8,128)S(1)} %bitcast.120) | data formatting | bytes 16777216 | tf_op jit(solution)/shard_map/while
  194.6 5.6 convolution_add_fusion.6
  208.2 5.3 convolution_add_fusion.7
  223.0 7.9 %copy.33 = f32[8,8,128,256]{3,1,2,0:T(8,128)} copy(f32[8,8,128,256]{3,2,1,0:T(8,128)S(1)} %bitcast.120) | data formatting | bytes 16777216 | tf_op jit(solution)/shard_map/while
  230.9 5.6 convolution_add_fusion.6
  244.5 5.3 convolution_add_fusion.7
  259.3 7.9 %copy.33 = f32[8,8,128,256]{3,1,2,0:T(8,128)} copy(f32[8,8,128,256]{3,2,1,0:T(8,128)S(1)} %bitcast.120) | data formatting | bytes 16777216 | tf_op jit(solution)/shard_map/while
  267.2 5.6 convolution_add_fusion.6
  280.8 5.3 convolution_add_fusion.7
  295.6 7.9 %copy.33 = f32[8,8,128,256]{3,1,2,0:T(8,128)} copy(f32[8,8,128,256]{3,2,1,0:T(8,128)S(1)} %bitcast.120) | data formatting | bytes 16777216 | tf_op jit(solution)/shard_map/while
  303.5 5.6 convolution_add_fusion.6
  317.1 5.3 convolution_add_fusion.7
  335.2 330.5 %psum.23 = f32[32,256]{1,0:T(8,128)S(1)} all-reduce(f32[32,256]{1,0:T(8,128)S(1)} %get-tuple-element.95), channel_id=1, replica_groups=mesh['row'=8,'col'=8,'tm'=2] {'row','col'}, use_global_device_ids=true, to_apply=%region_7.8 | all-reduce | flops 8192 | bytes 65536 | tf_op jit(solution)/shard_map/psum | solution.py:90
  (123 shorter events, 127.7 us)
Async XLA Ops:
  8.0 48.6 %all-gather.3.cloned.1.call-start = ((), (), s32[]{:S(2)}) async-start(), calls=%async_computation.2 | async-start | bytes 1114112 | tf_op jit(solution)/shard_map/all_gather | solution.py:20
  8.7 94.6 %all-gather.5.cloned.1.call-start = ((), (), s32[]{:S(2)}) async-start(), calls=%async_computation.3 | async-start | bytes 1114112 | tf_op jit(solution)/shard_map/all_gather | solution.py:19
  9.5 656.2 %all-reduce.3.cloned.1.call-start = ((), (), s32[]{:S(2)}) async-start(), calls=%async_computation.6 | async-start | bytes 1048576 | tf_op jit(solution)/shard_map/psum | solution.py:89
  13.2 654.4 %reduce-scatter.3.cloned.1.call-start = ((), (), s32[]{:S(2)}) async-start(), calls=%async_computation.4 | async-start | bytes 2228224 | tf_op jit(solution)/shard_map/reduce_scatter | solution.py:82
  25.3 80.4 %copy-start.2 = (bf16[32,256]{1,0:T(8,128)(2,1)S(1)}, bf16[32,256]{1,0:T(8,128)(2,1)}, u32[]{:S(2)}) copy-start(bf16[32,256]{1,0:T(8,128)(2,1)} %param.13) | copy-start | bytes 49156
  109.3 2.6 copy-start
  123.1 5.9 copy-start.1
  144.5 2.6 copy-start
  158.3 5.9 copy-start.1
  180.8 2.6 copy-start
  194.6 5.9 copy-start.1
  217.1 2.6 copy-start
  230.9 5.9 copy-start.1
  253.4 2.6 copy-start
  267.2 5.9 copy-start.1
  289.8 2.6 copy-start
  303.5 5.9 copy-start.1
  326.9 342.8 %reduce-scatter.5.cloned.1.call-start = ((), (), s32[]{:S(2)}) async-start(), calls=%async_computation.5 | async-start | bytes 2228224 | tf_op jit(solution)/shard_map/reduce_scatter | solution.py:83
  328.7 338.9 %copy-start.3 = (bf16[1,128,256]{2,1,0:T(8,128)(2,1)S(1)}, bf16[1,128,256]{2,1,0:T(8,128)(2,1)}, u32[]{:S(2)}) copy-start(bf16[1,128,256]{2,1,0:T(8,128)(2,1)} %param.11) | copy-start | bytes 196612
  328.7 341.1 %copy-start.4 = (bf16[1,128,256]{2,1,0:T(8,128)(2,1)S(1)}, bf16[1,128,256]{2,1,0:T(8,128)(2,1)}, u32[]{:S(2)}) copy-start(bf16[1,128,256]{2,1,0:T(8,128)(2,1)} %param.12) | copy-start | bytes 196612
Sparse Core Ops, SparseCore 0:
  11.2 45.3 all-gather.2
  58.4 44.9 all-gather.4
  327.0 70.3 reduce-scatter.2
  400.8 73.3 reduce-scatter.4
Sparse Core Ops, SparseCore 1:
  14.9 147.6 all-reduce.2
where the time goes:
time: 680 us; the launch traced here: 679 us
  blocking collectives  335 us (49%)
  matrix products  135 us (20%)
  local copies, waits for them, and re-layouts  103 us (15%)
  waiting for transfers between devices  77.9 us (11%)
  between operations  15.9 us (2%)
  other arithmetic  11.3 us (2%)
    psum x1, blocking collectives, on_device(): mttkrp_time = lax.psum(sum_time, ('row', 'col'))  331 us
    while x48, local copies, waits for them, and re-layouts  89.3 us
    all_gather x1, waiting for transfers between devices, on_device(): row_block = lax.all_gather(factor_rows, ('col', 'tm'), axis=1, tiled=True)  45.2 us
    dot_general x6, matrix products, add_block(): jnp.einsum('na,nx->ax', row_hot.astype(jnp.float32), row_terms, precision...  33.5 us
    all_gather x1, waiting for transfers between devices, on_device(): col_block = lax.all_gather(factor_cols, ('row', 'tm'), axis=1, tiled=True)  31.3 us
    dot_general x6, matrix products, add_block(): jnp.einsum('na,nx->ax', col_hot.astype(jnp.float32), col_terms, precision...  30.7 us
    dot_general x6, matrix products, add_block(): jnp.einsum('nij,njr->nir', block_vals, col_take, preferred_element_type=j...  19.4 us
    dot_general x6, matrix products, add_block(): jnp.einsum('nij,nir->njr', block_vals, row_take, preferred_element_type=j...  17.7 us
  transfers between devices with their start and end apart: 5, of which 2 were waited for; matrix products, arithmetic and copies ran while one was open for 36% of the time, Pallas kernels for 0%

commit v1 on v0

v1 whole, which is shorter than its diff:
```python
import jax
import jax.numpy as jnp
from jax import lax
from jax.experimental import pallas as pl
from jax.experimental.pallas import tpu as pltpu
from jax.sharding import PartitionSpec as P

F32 = jnp.float32
BF16 = jnp.bfloat16
I16 = jnp.int16
MESH = pl.DeviceIdType.MESH
EDGE = 128
RANK = 256
PAD = 16


class Net:
    def __init__(self, send, recv):
        self.send, self.recv, self.used, self.open = send, recv, 0, []

    def copy(self, src, dst, device):
        made = pltpu.make_async_remote_copy(
            src_ref=src,
            dst_ref=dst,
            send_sem=self.send.at[self.used],
            recv_sem=self.recv.at[self.used],
            device_id=device,
            device_id_type=MESH,
        )
        self.used += 1
        made.start()
        self.open.append(made)
        return made

    def close(self):
        for made in self.open:
            made.wait_send()


class Place:
    def __init__(self):
        row, col, self.t = lax.axis_index("row"), lax.axis_index("col"), lax.axis_index("tm")
        self.z, self.y, self.core = row // 2, col // 2, col % 2
        self.x = (row % 2) * 2 + self.t

    def at(self, dz=0, dy=0, dx=0, other=False):
        z, y, x = (self.z + dz) % 4, (self.y + dy) % 4, (self.x + dx) % 4
        core = 1 - self.core if other else self.core
        return (z * 2 + x // 2, y * 2 + core, x % 2)

    def pair(self):
        return (self.z * 2 + self.x // 2, self.y * 2 + self.core, 1 - self.t)

    def greet(self):
        barrier = pltpu.get_barrier_semaphore()
        others = [self.at(other=True)]
        for step in (1, 2, 3):
            others += [self.at(dz=step), self.at(dy=step), self.at(dx=step)]
        for device in others:
            pl.semaphore_signal(barrier, inc=1, device_id=device, device_id_type=MESH)
        pl.semaphore_wait(barrier, len(others))


def drive(*runs):
    runs = list(runs)
    while runs:
        for run in list(runs):
            if next(run, None) is None:
                runs.remove(run)


def ring_gather(net, view, half, me, plus, minus):
    up = net.copy(view(me), view(me), plus)
    down = net.copy(view(me), view(me), minus)
    yield 1
    before, after = (me + 3) % 4, (me + 1) % 4
    up.wait_recv()
    up = net.copy(half(before, 0), half(before, 0), plus)
    down.wait_recv()
    down = net.copy(half(after, 1), half(after, 1), minus)
    yield 1
    up.wait_recv()
    down.wait_recv()


def spread(net, view, me, devices):
    made = [net.copy(view(me), view(me), device) for device in devices]
    yield 1
    for copy in made:
        copy.wait_recv()


def swap(net, src, dst, device):
    made = net.copy(src, dst, device)
    yield 1
    made.wait_recv()


def encode(wire, value):
    rows = value.shape[0]
    top = jnp.max(jnp.abs(value), axis=0, keepdims=True)
    power = jnp.ceil(jnp.log2(jnp.maximum(top, 1e-30)))
    coded = jnp.clip(value * jnp.exp2(15.0 - power), -32767.0, 32767.0)
    wire[0:rows] = jnp.round(coded).astype(jnp.int32).astype(I16)
    wire[rows : rows + PAD] = jnp.broadcast_to(power, (PAD, RANK)).astype(jnp.int32).astype(I16)


def decode(wire):
    rows = wire.shape[0] - PAD
    power = wire[rows : rows + PAD].astype(jnp.int32).astype(F32)[0:1]
    return wire[0:rows].astype(jnp.int32).astype(F32) * jnp.exp2(power - 15.0)


def ring_reduce(net, src, me, plus, minus, sent, got, out):
    after, far, before = (me + 1) % 4, (me + 2) % 4, (me + 3) % 4
    encode(sent.at[0], src(far, 0))
    relay_up = net.copy(sent.at[0], got.at[0], plus)
    encode(sent.at[1], src(far, 1))
    relay_down = net.copy(sent.at[1], got.at[1], minus)
    encode(sent.at[2], src(after, 1))
    own_up = net.copy(sent.at[2], got.at[2], plus)
    encode(sent.at[3], src(before, 0))
    own_down = net.copy(sent.at[3], got.at[3], minus)
    yield 1
    relay_up.wait_recv()
    encode(sent.at[4], decode(got.at[0]) + src(after, 0))
    sum_up = net.copy(sent.at[4], got.at[4], plus)
    relay_down.wait_recv()
    encode(sent.at[5], decode(got.at[1]) + src(before, 1))
    sum_down = net.copy(sent.at[5], got.at[5], minus)
    yield 1
    for copy in (own_up, own_down, sum_up, sum_down):
        copy.wait_recv()
    out(0, src(me, 0) + decode(got.at[4]) + decode(got.at[3]))
    out(1, src(me, 1) + decode(got.at[2]) + decode(got.at[5]))


def gather_rows(net, at, full):
    yield from swap(net, full.at[at.y, at.core, at.t], full.at[at.y, at.core, at.t], at.pair())
    yield from ring_gather(
        net,
        lambda p: full.at[p, at.core],
        lambda p, h: full.at[p, at.core, h],
        at.y,
        at.at(dy=1),
        at.at(dy=3),
    )
    yield from swap(net, full.at[:, at.core], full.at[:, at.core], at.at(other=True))


def gather_cols_low(net, at, full):
    yield from ring_gather(
        net,
        lambda p: full.at[p, at.x, 0:64],
        lambda p, h: full.at[p, at.x, 32 * h : 32 * h + 32],
        at.z,
        at.at(dz=1),
        at.at(dz=3),
    )
    yield from ring_gather(
        net,
        lambda p: full.at[:, p, 0:64],
        lambda p, h: full.at[2 * h : 2 * h + 2, p, 0:64],
        at.x,
        at.at(dx=1),
        at.at(dx=3),
    )


def gather_cols_high(net, at, full):
    yield from ring_gather(
        net,
        lambda p: full.at[at.z, p, 64:128],
        lambda p, h: full.at[at.z, p, 64 + 32 * h : 96 + 32 * h],
        at.x,
        at.at(dx=1),
        at.at(dx=3),
    )
    yield from ring_gather(
        net,
        lambda p: full.at[p, :, 64:128],
        lambda p, h: full.at[p, 2 * h : 2 * h + 2, 64:128],
        at.z,
        at.at(dz=1),
        at.at(dz=3),
    )


def gather_kernel(rows, cols, times, a_full, b_full, c_full, send, recv):
    at = Place()
    net = Net(send, recv)
    a_full[at.y, at.core, at.t] = rows[0]
    b_full[at.z, at.x] = cols[0]
    c_full[at.t] = times[...]
    at.greet()
    drive(
        gather_cols_low(net, at, b_full),
        gather_cols_high(net, at, b_full),
        gather_rows(net, at, a_full),
        swap(net, c_full.at[at.t], c_full.at[at.t], at.pair()),
    )
    net.close()


LOADS = 12
UNROLL = 4


def tile_kernel(coords, count, values, a, b, times, sum_a, sum_b, sum_c, held, ctime, sems):
    slots = values.shape[0]
    part = slots // LOADS

    def load(i):
        span = pl.ds(i * part, part)
        return pltpu.make_async_copy(values.at[span], held.at[span], sems.at[i])

    for i in range(LOADS):
        load(i).start()
    sum_a[...] = jnp.zeros_like(sum_a)
    sum_b[...] = jnp.zeros_like(sum_b)
    sum_c[...] = jnp.zeros_like(sum_c)
    ctime[...] = times[...].astype(F32)
    live = count[0]

    def one(s):
        row, col, snap = coords[0, s], coords[1, s], coords[2, s]
        tile = held[s]
        a_here = a[row]
        prod = jnp.dot(tile, b[col], preferred_element_type=F32)
        back = lax.dot_general(tile, a_here, (((0,), (0,)), ((), ())), preferred_element_type=F32)
        scale = jnp.where(s < live, ctime[pl.ds(snap, 1), :], 0.0)
        mask = jnp.where(s < live, 1.0, 0.0)
        here = jnp.sum(a_here.astype(F32) * prod, axis=0, keepdims=True) * mask
        return row, col, snap, prod * scale, back * scale, here

    for i in range(LOADS):
        load(i).wait()

        @pl.loop(i * part, (i + 1) * part, step=UNROLL)
        def _(first):
            found = [one(first + u) for u in range(UNROLL)]
            for row, col, snap, to_row, to_col, here in found:
                sum_a[row] += to_row
                sum_b[col] += to_col
                sum_c[pl.ds(snap, 1), :] += here


def reduce_rows(net, at, part, chip, pair_sum, total, core_s, core_r, y_s, y_r, x_s, x_r):
    made = []
    order = [(at.y + step) % 4 for step in (2, 1, 3, 0)]
    for p in order:
        for h in range(2):
            encode(core_s.at[p, h], part[p, 1 - at.core, h])
        made.append(net.copy(core_s.at[p], core_r.at[p], at.at(other=True)))
    yield 1
    for p, copy in zip(order, made):
        copy.wait_recv()
        for h in range(2):
            chip[p, h] = part[p, at.core, h] + decode(core_r.at[p, h])

    def out(h, value):
        pair_sum[h] = value

    yield from ring_reduce(
        net, lambda p, h: chip[p, h], at.y, at.at(dy=1), at.at(dy=3), y_s, y_r, out
    )
    encode(x_s, pair_sum[1 - at.t])
    yield from swap(net, x_s, x_r, at.pair())
    total[...] = pair_sum[at.t] + decode(x_r)


def reduce_cols_low(net, at, part, mid, total, s1, r1, s2, r2):
    def out_mid(h, value):
        mid[2 * h : 2 * h + 2] = value.reshape(2, 64, RANK)

    def out(h, value):
        total[32 * h : 32 * h + 32] = value

    yield from ring_reduce(
        net,
        lambda p, h: part[2 * h : 2 * h + 2, p, 0:64].reshape(EDGE, RANK),
        at.x,
        at.at(dx=1),
        at.at(dx=3),
        s1,
        r1,
        out_mid,
    )
    yield from ring_reduce(
        net,
        lambda p, h: mid[p, 32 * h : 32 * h + 32],
        at.z,
        at.at(dz=1),
        at.at(dz=3),
        s2,
        r2,
        out,
    )


def reduce_cols_high(net, at, part, mid, total, s1, r1, s2, r2):
    def out_mid(h, value):
        mid[2 * h : 2 * h + 2] = value.reshape(2, 64, RANK)

    def out(h, value):
        total[64 + 32 * h : 96 + 32 * h] = value

    yield from ring_reduce(
        net,
        lambda p, h: part[p, 2 * h : 2 * h + 2, 64:128].reshape(EDGE, RANK),
        at.z,
        at.at(dz=1),
        at.at(dz=3),
        s1,
        r1,
        out_mid,
    )
    yield from ring_reduce(
        net,
        lambda p, h: mid[p, 32 * h : 32 * h + 32],
        at.x,
        at.at(dx=1),
        at.at(dx=3),
        s2,
        r2,
        out,
    )


def along(at, name):
    return [at.at(**{name: step}) for step in (1, 2, 3)]


def sum_four(ref):
    return (ref[0] + ref[1]) + (ref[2] + ref[3])


def gram_rows(net, at, whole, four, two, full):
    block = (at.y * 4 + at.core * 2 + at.t) * 16
    four[at.z] = whole[pl.ds(pl.multiple_of(block, 16), 16), :]
    yield from spread(net, lambda p: four.at[p], at.z, along(at, "dz"))
    two[0] = sum_four(four)
    yield from swap(net, two.at[0], two.at[1], at.at(dx=2))
    full[at.y, at.core, at.t] = two[0] + two[1]
    yield from swap(net, full.at[at.y, at.core, at.t], full.at[at.y, at.core, at.t], at.pair())
    yield from spread(net, lambda p: full.at[p, at.core], at.y, along(at, "dy"))
    yield from swap(net, full.at[:, at.core], full.at[:, at.core], at.at(other=True))


def gram_cols(net, at, whole, four, two, full):
    block = (at.z * 4 + at.x) * 16
    four[at.y] = whole[pl.ds(pl.multiple_of(block, 16), 16), :]
    yield from spread(net, lambda p: four.at[p], at.y, along(at, "dy"))
    two[0] = sum_four(four)
    yield from swap(net, two.at[0], two.at[1], at.at(other=True))
    full[at.z, at.x] = two[0] + two[1]
    yield from spread(net, lambda p: full.at[p, at.x], at.z, along(at, "dz"))
    yield from spread(net, lambda p: full.at[:, p], at.x, along(at, "dx"))


def reduce_time(net, at, part, four_y, two_y, four_z, two_z, total):
    four_y[at.y] = part[...]
    yield from spread(net, lambda p: four_y.at[p], at.y, along(at, "dy"))
    two_y[0] = sum_four(four_y)
    yield from swap(net, two_y.at[0], two_y.at[1], at.at(other=True))
    four_z[at.z] = two_y[0] + two_y[1]
    yield from spread(net, lambda p: four_z.at[p], at.z, along(at, "dz"))
    two_z[0] = sum_four(four_z)
    yield from swap(net, two_z.at[0], two_z.at[1], at.at(dx=2))
    total[...] = two_z[0] + two_z[1]


def exact_dot(left, right):
    high = right.astype(BF16)
    rest = right - high.astype(F32)
    mid = rest.astype(BF16)
    low = (rest - mid.astype(F32)).astype(BF16)
    return (
        jnp.dot(left, low, preferred_element_type=F32)
        + jnp.dot(left, mid, preferred_element_type=F32)
        + jnp.dot(left, high, preferred_element_type=F32)
    )


def gram(ref):
    block = ref[...]
    return lax.dot_general(block, block, (((0,), (0,)), ((), ())), preferred_element_type=F32)


def reduce_kernel(
    sum_a, sum_b, sum_c, a_full, b_full, c_full, grad_a, grad_b, grad_c, s, send, recv
):
    at = Place()
    net = Net(send, recv)
    a_flat = a_full.reshape(16, EDGE, RANK)
    b_flat = b_full.reshape(16, EDGE, RANK)
    at.greet()
    runs = [
        reduce_rows(
            net, at, sum_a, s["chip"], s["pair"], s["total_a"],
            s["core_s"], s["core_r"], s["y_s"], s["y_r"], s["x_s"], s["x_r"],
        ),
        reduce_cols_low(
            net, at, sum_b, s["mid0"], s["total_b"], s["l1_s"], s["l1_r"], s["l2_s"], s["l2_r"]
        ),
        reduce_cols_high(
            net, at, sum_b, s["mid1"], s["total_b"], s["h1_s"], s["h1_r"], s["h2_s"], s["h2_r"]
        ),
    ]
    for run in runs:
        next(run)
    s["gram_a"][...] = jnp.zeros((RANK, RANK), F32)
    s["gram_b"][...] = jnp.zeros((RANK, RANK), F32)

    @pl.loop(0, 16)
    def _(i):
        s["gram_a"][...] += gram(a_flat.at[i])
        s["gram_b"][...] += gram(b_flat.at[i])

    runs += [
        gram_rows(net, at, s["gram_a"], s["ga4"], s["ga2"], s["ga"]),
        gram_cols(net, at, s["gram_b"], s["gb4"], s["gb2"], s["gb"]),
        reduce_time(net, at, sum_c, s["cy4"], s["cy2"], s["cz4"], s["cz2"], s["total_c"]),
    ]
    drive(*runs)
    whole_a = s["ga"][...].reshape(RANK, RANK)
    whole_b = s["gb"][...].reshape(RANK, RANK)
    c_all = c_full[...].reshape(2 * c_full.shape[1], RANK)
    whole_c = lax.dot_general(c_all, c_all, (((0,), (0,)), ((), ())), preferred_element_type=F32)
    grad_a[0] = exact_dot(a_full[at.y, at.core, at.t], whole_b * whole_c) - s["total_a"][...]
    grad_b[0] = exact_dot(b_full[at.z, at.x], whole_a * whole_c) - s["total_b"][...]
    grad_c[...] = exact_dot(c_full[at.t], whole_a * whole_b) - s["total_c"][...]
    net.close()


def vmem(count):
    return [pl.BlockSpec(memory_space=pltpu.VMEM)] * count


def on_device(tile_values, tile_coords, tile_counts, factor_rows, factor_cols, factor_time):
    values = tile_values[0, 0, 0]
    coords = tile_coords[0, 0, 0]
    count = tile_counts.reshape(1)
    section = factor_time.shape[0]
    slots = values.shape[0]
    sds = jax.ShapeDtypeStruct
    copies = 32
    a_full, b_full, c_full = pl.pallas_call(
        gather_kernel,
        out_shape=(
            sds((4, 2, 2, EDGE, RANK), BF16),
            sds((4, 4, EDGE, RANK), BF16),
            sds((2, section, RANK), BF16),
        ),
        in_specs=vmem(3),
        out_specs=tuple(vmem(3)),
        scratch_shapes=[pltpu.SemaphoreType.DMA((copies,)), pltpu.SemaphoreType.DMA((copies,))],
        compiler_params=pltpu.CompilerParams(
            collective_id=0, has_side_effects=True, vmem_limit_bytes=48 << 20
        ),
        name="gather",
    )(factor_rows, factor_cols, factor_time)
    smem = pl.BlockSpec(memory_space=pltpu.SMEM)
    sum_a, sum_b, sum_c = pl.pallas_call(
        tile_kernel,
        out_shape=(
            sds((16, EDGE, RANK), F32),
            sds((16, EDGE, RANK), F32),
            sds((section, RANK), F32),
        ),
        in_specs=[smem, smem, pl.BlockSpec(memory_space=pl.ANY)] + vmem(3),
        out_specs=tuple(vmem(3)),
        scratch_shapes=[
            pltpu.VMEM((slots, EDGE, EDGE), BF16),
            pltpu.VMEM((section, RANK), F32),
            pltpu.SemaphoreType.DMA((LOADS,)),
        ],
        compiler_params=pltpu.CompilerParams(vmem_limit_bytes=56 << 20),
        name="tiles",
    )(
        coords,
        count,
        values,
        a_full.reshape(16, EDGE, RANK),
        b_full.reshape(16, EDGE, RANK),
        factor_time,
    )
    wire = lambda *lead: pltpu.VMEM(lead + (RANK,), I16)
    held = lambda *lead: pltpu.VMEM(lead + (RANK,), F32)
    big, small = EDGE + PAD, 32 + PAD
    scratch = dict(
        chip=held(4, 2, EDGE), pair=held(2, EDGE), total_a=held(EDGE), total_b=held(EDGE),
        core_s=wire(4, 2, big), core_r=wire(4, 2, big),
        y_s=wire(6, big), y_r=wire(6, big), x_s=wire(big), x_r=wire(big),
        mid0=held(4, 64), mid1=held(4, 64),
        l1_s=wire(6, big), l1_r=wire(6, big), l2_s=wire(6, small), l2_r=wire(6, small),
        h1_s=wire(6, big), h1_r=wire(6, big), h2_s=wire(6, small), h2_r=wire(6, small),
        gram_a=held(RANK), gram_b=held(RANK),
        ga4=held(4, 16), ga2=held(2, 16), ga=held(4, 2, 2, 16),
        gb4=held(4, 16), gb2=held(2, 16), gb=held(4, 4, 16),
        cy4=held(4, section), cy2=held(2, section), cz4=held(4, section), cz2=held(2, section),
        total_c=held(section),
    )
    copies = 96
    return pl.pallas_call(
        reduce_kernel,
        out_shape=(
            sds((1, EDGE, RANK), F32),
            sds((1, EDGE, RANK), F32),
            sds((section, RANK), F32),
        ),
        in_specs=vmem(6),
        out_specs=tuple(vmem(3)),
        scratch_shapes=[
            scratch,
            pltpu.SemaphoreType.DMA((copies,)),
            pltpu.SemaphoreType.DMA((copies,)),
        ],
        compiler_params=pltpu.CompilerParams(
            collective_id=1, has_side_effects=True, vmem_limit_bytes=56 << 20
        ),
        name="reduce",
    )(
        sum_a.reshape(4, 2, 2, EDGE, RANK),
        sum_b.reshape(4, 4, EDGE, RANK),
        sum_c,
        a_full,
        b_full,
        c_full,
    )


def solution(mesh):
    return jax.shard_map(
        on_device,
        mesh=mesh,
        in_specs=(
            P("row", "col", "tm", None, None, None),
            P("row", "col", "tm", None, None),
            P("row", "col", "tm"),
            P("row", ("col", "tm"), None),
            P("col", ("row", "tm"), None),
            P("tm", None),
        ),
        out_specs=(P("row", ("col", "tm"), None), P("col", ("row", "tm"), None), P("tm", None)),
        check_vma=False,
    )
```

time: 680 us -> 104 us (0.15)
  blocking collectives: 335 us -> 0 us
  matrix products: 135 us -> 0 us
  local copies, waits for them, and re-layouts: 103 us -> 10.8 us
  Pallas kernels: 0 us -> 90.4 us
  waiting for transfers between devices: 77.9 us -> 0 us
  between operations: 15.9 us -> 1.32 us
  other arithmetic: 11.3 us -> 0 us
    psum x1 -> x0, blocking collectives: 331 us -> none  [on_device(): mttkrp_time = lax.psum(sum_time, ('row', 'col'))]
    dot_general x54 -> x0, matrix products: 135 us -> none  [the longest x6 33.5 us: add_block(): jnp.einsum('na,nx->ax', row_hot.astype(jnp.float32), row_terms, precision...]
    pallas_call x0 -> x3, Pallas kernels: none -> 90.4 us  [the longest x1 35 us: on_device(): pl.pallas_call(tile_kernel, out_shape=(sds((16, EDGE, RANK), F32), sds((1...]
    while x48 -> x0, local copies, waits for them, and re-layouts: 89.3 us -> none
    all_gather x2 -> x0, waiting for transfers between devices: 76.5 us -> none  [the longest x1 45.2 us: on_device(): row_block = lax.all_gather(factor_rows, ('col', 'tm'), axis=1, tiled=True)]
    select_n x1 -> x0, other arithmetic: 10.6 us -> none  [on_device(): jnp.where(live_slots[:, None, None], tile_vals, jnp.zeros((), tile_vals.d...]
    unnamed x8 -> x16, local copies, waits for them, and re-layouts: 1.53 us -> 10.8 us
    reshape x4 -> x0, local copies, waits for them, and re-layouts: 7.96 us -> none  [the longest x2 4.41 us: on_device(): sum_rows = sum_rows.reshape(1, -1, rank_width)]
  transfers between devices with their start and end apart: 5 -> 0, of which waited for: 2 -> 0; matrix products, arithmetic and copies ran while one was open for 36% -> 0% of each run, Pallas kernels for 0% -> 0%
where the time goes in v1:
time: 104 us; the launch traced here: 102 us
  Pallas kernels  90.4 us (87%)
  local copies, waits for them, and re-layouts  10.8 us (10%)
  between operations  1.32 us (1%)
    pallas_call x1, Pallas kernels, on_device(): pl.pallas_call(tile_kernel, out_shape=(sds((16, EDGE, RANK), F32), sds((1...  35 us
    pallas_call x1, Pallas kernels, on_device(): pl.pallas_call(reduce_kernel, out_shape=(sds((1, EDGE, RANK), F32), sds((...  31.7 us
    pallas_call x1, Pallas kernels, on_device(): pl.pallas_call(gather_kernel, out_shape=(sds((4, 2, 2, EDGE, RANK), BF16)...  23.7 us
    unnamed x16, local copies, waits for them, and re-layouts  10.8 us

profile of v1, /device:TPU:0, one launch (start us, length us, event | category | flops | bytes accessed | tf_op | source)
XLA Modules:
  0.0 102.4 jit_solution(15215996500936297267)
XLA Ops:
  1.3 1.3 %copy.11 = s32[1,1,1,3,384]{4,3,2,1,0:T(4,128)} copy(s32[1,1,1,3,384]{4,2,3,1,0:T(1,128)} %param.7) | data formatting | bytes 9216
  2.6 0.0 copy-start.2
  2.6 0.7 copy-done.2
  3.3 0.0 copy-start.3
  3.3 0.8 copy-done.3
  4.1 0.0 copy-start.4
  4.1 0.8 copy-done.4
  5.0 23.7 %gather.1 = (bf16[4,2,2,128,256]{4,3,2,1,0:T(8,128)(2,1)S(1)}, bf16[4,4,128,256]{3,2,1,0:T(8,128)(2,1)S(1)}, bf16[2,32,256]{2,1,0:T(8,128)(2,1)S(1)}) custom-call(bf16[1,128,256]{2,1,0:T(8,128)(2,1)S(1)} %copy-done.3, bf16[1,128,256]{2,1,0:T(8,128)(2,1)S(1)} %copy-done.4, bf16[32,256]{1,0:T(8,128)(2,1)S(1)} %copy-done.2), custom_call_target="tpu_custom_call" | custom-call | tf_op jit(solution)/shard_map/gather/pallas_call | solution.py:448
  28.6 0.0 copy-start
  28.6 1.0 copy-done
  29.6 0.0 copy-start.1
  29.6 1.0 copy-done.1
  30.6 0.0 copy-start.5
  30.6 0.6 copy-done.5
  31.2 35.0 %tiles.1 = (f32[16,128,256]{2,1,0:T(8,128)}, f32[16,128,256]{2,1,0:T(8,128)}, f32[32,256]{1,0:T(8,128)}) custom-call(s32[3,384]{1,0:T(4,128)} %bitcast.15, s32[1]{0:T(128)} %bitcast.9.count, bf16[384,128,128]{2,1,0:T(8,128)(2,1)} %bitcast.12, bf16[16,128,256]{2,1,0:T(8,128)(2,1)} %bitcast.10, bf16[16,128,256]{2,1,0:T(8,128)(2,1)} %bitcast.11, ...), custom_call_target="tpu_custom_call" | custom-call | tf_op jit(solution)/shard_map/tiles/pallas_call | solution.py:464
  66.3 31.7 %reduce.1 = (f32[1,128,256]{2,1,0:T(8,128)}, f32[1,128,256]{2,1,0:T(8,128)}, f32[32,256]{1,0:T(8,128)}) custom-call(f32[4,2,2,128,256]{4,3,2,1,0:T(8,128)} %bitcast.13, f32[4,4,128,256]{3,2,1,0:T(8,128)} %bitcast.14, f32[32,256]{1,0:T(8,128)} %get-tuple-element.13.sum_c, bf16[4,2,2,128,256]{4,3,2,1,0:T(8,128)(2,1)} %copy-done, ...), custom_call_target="tpu_custom_call" | custom-call | tf_op jit(solution)/shard_map/reduce/pallas_call | solution.py:505
  97.9 1.6 %copy.16 = f32[1,128,256]{2,1,0:T(8,128)} copy(f32[1,128,256]{2,1,0:T(8,128)} %get-tuple-element.18) | data formatting | bytes 262144
  99.5 1.6 %copy.17 = f32[1,128,256]{2,1,0:T(8,128)} copy(f32[1,128,256]{2,1,0:T(8,128)} %get-tuple-element.19) | data formatting | bytes 262144
  101.1 1.4 %copy.18 = f32[32,256]{1,0:T(8,128)} copy(f32[32,256]{1,0:T(8,128)} %get-tuple-element.20) | data formatting | bytes 65536
Async XLA Ops:
  2.6 0.7 copy-start.2
  3.3 0.8 copy-start.3
  4.1 0.8 copy-start.4
  28.6 1.0 copy-start
  29.6 1.0 copy-start.1
  30.6 0.6 copy-start.5

commit v2 on v0

v2 whole, which is shorter than its diff:
```python
import jax
import jax.numpy as jnp
from jax import lax
from jax.experimental import pallas as pl
from jax.experimental.pallas import tpu as pltpu
from jax.sharding import PartitionSpec as P

F32 = jnp.float32
BF16 = jnp.bfloat16
I16 = jnp.int16
MESH = pl.DeviceIdType.MESH
EDGE = 128
RANK = 256
PAD = 16


class Net:
    def __init__(self, send, recv):
        self.send, self.recv, self.used, self.open = send, recv, 0, []

    def copy(self, src, dst, device):
        made = pltpu.make_async_remote_copy(
            src_ref=src,
            dst_ref=dst,
            send_sem=self.send.at[self.used],
            recv_sem=self.recv.at[self.used],
            device_id=device,
            device_id_type=MESH,
        )
        self.used += 1
        made.start()
        self.open.append(made)
        return made

    def close(self):
        for made in self.open:
            made.wait_send()


class Place:
    def __init__(self):
        row, col, self.t = lax.axis_index("row"), lax.axis_index("col"), lax.axis_index("tm")
        self.z, self.y, self.core = row // 2, col // 2, col % 2
        self.x = (row % 2) * 2 + self.t

    def at(self, dz=0, dy=0, dx=0, other=False):
        z, y, x = (self.z + dz) % 4, (self.y + dy) % 4, (self.x + dx) % 4
        core = 1 - self.core if other else self.core
        return (z * 2 + x // 2, y * 2 + core, x % 2)

    def pair(self):
        return (self.z * 2 + self.x // 2, self.y * 2 + self.core, 1 - self.t)

    def greet(self):
        barrier = pltpu.get_barrier_semaphore()
        others = [self.at(other=True)]
        for step in (1, 2, 3):
            others += [self.at(dz=step), self.at(dy=step), self.at(dx=step)]
        for device in others:
            pl.semaphore_signal(barrier, inc=1, device_id=device, device_id_type=MESH)
        pl.semaphore_wait(barrier, len(others))


def drive(*runs):
    runs = list(runs)
    while runs:
        for run in list(runs):
            if next(run, None) is None:
                runs.remove(run)


def spread(net, view, me, devices):
    made = [net.copy(view(me), view(me), device) for device in devices]
    yield 1
    for copy in made:
        copy.wait_recv()


def swap(net, src, dst, device):
    made = net.copy(src, dst, device)
    yield 1
    made.wait_recv()


def encode(wire, value):
    rows = value.shape[0]
    top = jnp.max(jnp.abs(value), axis=0, keepdims=True)
    power = jnp.ceil(jnp.log2(jnp.maximum(top, 1e-30)))
    coded = jnp.clip(value * jnp.exp2(15.0 - power), -32767.0, 32767.0)
    wire[0:rows] = jnp.round(coded).astype(jnp.int32).astype(I16)
    power = jnp.broadcast_to(power, (PAD, value.shape[1]))
    wire[rows : rows + PAD] = power.astype(jnp.int32).astype(I16)


def decode(wire):
    rows = wire.shape[0] - PAD
    power = wire[rows : rows + PAD].astype(jnp.int32).astype(F32)[0:1]
    return wire[0:rows].astype(jnp.int32).astype(F32) * jnp.exp2(power - 15.0)


SLOTS = 384
ROUND = 2
PADDED = SLOTS + 16 * (ROUND - 1)
ROUNDS = PADDED // ROUND
LANES = 512
UNROLL = 40
LOADS = 12


def iota(shape, dim):
    return lax.broadcasted_iota(jnp.int32, shape, dim)


def up_to_round(n):
    return (n + (ROUND - 1)) // ROUND * ROUND


def lane_sum(value):
    return jnp.sum(value.astype(F32), axis=1, keepdims=True).astype(jnp.int32)


def plan_groups(plan, line, key_row, key_col, entry):
    lane = iota((1, 128), 1)
    count = jnp.sum((key_col == lane).astype(jnp.int32), axis=0, keepdims=True)
    padded = up_to_round(count)
    group = iota((16, 128), 0)
    held = jnp.zeros((16, 128), jnp.int32)
    for m in range(SLOTS // 128):
        held += (key_row[:, 128 * m : 128 * m + 128] == group).astype(jnp.int32)
    tall = up_to_round(lane_sum(held))
    end = jnp.sum(jnp.where(group <= iota((16, 128), 1), tall, 0), axis=0, keepdims=True)
    plan[line + 1 : line + 2, 0:128] = jnp.clip((end - padded) // ROUND, 0, ROUNDS)
    plan[line + 2 : line + 3, 0:128] = jnp.clip(end // ROUND, 0, ROUNDS)
    found = [jnp.zeros((1, 128), jnp.int32) for _ in range(LANES // 128)]
    for c in range(SLOTS // 128):
        mine = key_col[128 * c : 128 * c + 128]
        before = jnp.where(iota((128, 128), 1) < mine, padded, 0)
        for m in range(SLOTS // 128):
            same = key_row[:, 128 * m : 128 * m + 128] == mine
            earlier = iota((128, 128), 1) + 128 * m < iota((128, 128), 0) + 128 * c
            before += (same & earlier).astype(jnp.int32)
        place = lane_sum(before)
        told = entry[128 * c : 128 * c + 128]
        for q in range(LANES // 128):
            hit = place == iota((128, 128), 1) + 128 * q
            found[q] += jnp.sum(jnp.where(hit, told, 0), axis=0, keepdims=True)
    for q in range(LANES // 128):
        plan[line : line + 1, 128 * q : 128 * q + 128] = found[q]


def make_plan(plan, coords, live):
    rows, cols, snaps = coords[0], coords[1], coords[2]
    slot = iota((1, SLOTS), 1)
    row = jnp.where(slot < live, snaps + 32, 0)
    entry = slot + rows * 512 + cols * 8192 + row * 131072
    tall = jnp.concatenate(
        [jnp.broadcast_to(entry[:, 128 * c : 128 * c + 128], (128, 128)).T for c in range(3)],
        axis=0,
    )
    plan_groups(plan, 0, rows, (tall >> 9) & 15, tall)
    plan_groups(plan, 3, cols, (tall >> 13) & 15, tall)


def gather_rows(net, at, full):
    own = full.at[at.y, at.core, at.t]
    pair = net.copy(own, own, at.pair())
    mine = [net.copy(own, own, at.at(dy=k)) for k in (1, 3, 2)]
    yield 1
    pair.wait_recv()
    other = full.at[at.y, at.core, 1 - at.t]
    far = [net.copy(other, other, at.at(dy=k)) for k in (1, 3, 2)]
    near = full.at[at.y, at.core]
    across = [net.copy(near, near, at.at(other=True))]
    yield 1
    for k, first, second in zip((1, 3, 2), mine, far):
        first.wait_recv()
        second.wait_recv()
        came = full.at[(at.y + 4 - k) % 4, at.core]
        across.append(net.copy(came, came, at.at(other=True)))
    yield 1
    for copy in across:
        copy.wait_recv()


def gather_cols(net, at, full):
    def low(z):
        return full.at[z, at.x, 0:64]

    def high(x):
        return full.at[at.z, x, 64:128]

    order = (1, 3, 2)
    low_in = [net.copy(low(at.z), low(at.z), at.at(dz=k)) for k in order]
    high_in = [net.copy(high(at.x), high(at.x), at.at(dx=k)) for k in order]
    rest = []
    for k in order:
        rest.append(net.copy(low(at.z), low(at.z), at.at(dx=k)))
        rest.append(net.copy(high(at.x), high(at.x), at.at(dz=k)))
    yield 1
    for k, from_z, from_x in zip(order, low_in, high_in):
        from_z.wait_recv()
        came = low((at.z + 4 - k) % 4)
        rest += [net.copy(came, came, at.at(dx=j)) for j in order]
        from_x.wait_recv()
        came = high((at.x + 4 - k) % 4)
        rest += [net.copy(came, came, at.at(dz=j)) for j in order]
    yield 1
    for copy in rest:
        copy.wait_recv()


def tile_pass(plan, line, trips, held, times, operand, turned, prefix, other=None, dots=None):
    key = 13 if line == 0 else 9
    back = 9 if line == 0 else 13

    @pl.loop(*trips)
    def _(trip):
        total = prefix[trip * (UNROLL // ROUND)]
        for j in range(UNROLL // ROUND):
            for u in range(ROUND):
                place = trip * UNROLL + j * ROUND + u
                entry = plan[line, place]
                tile = held[jnp.minimum(entry & 511, SLOTS - 1)]
                dims = (((0,), (0,)), ((), ())) if turned else (((1,), (0,)), ((), ()))
                prod = lax.dot_general(
                    tile, operand[(entry >> key) & 15], dims, preferred_element_type=F32
                )
                total = total + prod * times[pl.ds((entry >> 17) & 63, 1), :]
                if dots is not None:
                    facing = other[(entry >> back) & 15].astype(F32)
                    dots[pl.ds(place, 1), :] = jnp.sum(facing * prod, axis=0, keepdims=True)
            prefix[trip * (UNROLL // ROUND) + j + 1] = total


def reduce_rows(net, at, block, chip, total, s):
    order = (2, 1, 3, 0)
    made = {}
    for k in order:
        y = (at.y + k) % 4
        for h in range(2):
            encode(s["core_s"].at[k, h], block(y, 1 - at.core, h))
        made[k] = net.copy(s["core_s"].at[k], s["core_r"].at[k], at.at(other=True))
    for k in order:
        y = (at.y + k) % 4
        for h in range(2):
            chip[k, h] = block(y, at.core, h)
    yield 1
    sent = {}
    for k in order:
        made[k].wait_recv()
        for h in range(2):
            value = chip[k, h] + decode(s["core_r"].at[k, h])
            if k:
                encode(s["y_s"].at[k, h], value)
            else:
                chip[0, h] = value
        if k:
            sent[k] = net.copy(s["y_s"].at[k], s["y_r"].at[k], at.at(dy=k))
    yield 1
    for k in (1, 3, 2):
        sent[k].wait_recv()
        for h in range(2):
            chip[0, h] += decode(s["y_r"].at[k, h])
    encode(s["x_s"], chip[0, 1 - at.t])
    yield from swap(net, s["x_s"], s["x_r"], at.pair())
    total[...] = chip[0, at.t] + decode(s["x_r"])


def reduce_cols(net, at, block, first, second, here, total, s1, r1, s2, r2):
    order = (2, 1, 3, 0)
    made = {}
    for k in order:
        for j in (2, 1, 3):
            encode(s1.at[k, j], block(k, j))
            made[k, j] = net.copy(s1.at[k, j], r1.at[k, j], at.at(**{first: j}))
        yield 1
    sent = {}
    for k in order:
        for j in (1, 3, 2):
            made[k, j].wait_recv()
        value = block(k, 0)
        for j in (1, 3, 2):
            value = value + decode(r1.at[k, j])
        if k:
            encode(s2.at[k], value)
            sent[k] = net.copy(s2.at[k], r2.at[k], at.at(**{second: k}))
        else:
            here[...] = value
        yield 1
    value = here[...]
    for k in (2, 1, 3):
        sent[k].wait_recv()
        value = value + decode(r2.at[k])
    total(value)


def along(at, name):
    return [at.at(**{name: step}) for step in (1, 2, 3)]


def sum_four(ref):
    return (ref[0] + ref[1]) + (ref[2] + ref[3])


def gram_rows(net, at, whole, four, two, full):
    block = (at.y * 4 + at.core * 2 + at.t) * 16
    four[at.z] = whole[pl.ds(pl.multiple_of(block, 16), 16), :]
    yield from spread(net, lambda p: four.at[p], at.z, along(at, "dz"))
    two[0] = sum_four(four)
    yield from swap(net, two.at[0], two.at[1], at.at(dx=2))
    full[at.y, at.core, at.t] = two[0] + two[1]
    yield from swap(net, full.at[at.y, at.core, at.t], full.at[at.y, at.core, at.t], at.pair())
    yield from spread(net, lambda p: full.at[p, at.core], at.y, along(at, "dy"))
    yield from swap(net, full.at[:, at.core], full.at[:, at.core], at.at(other=True))


def gram_cols(net, at, whole, four, two, full):
    block = (at.z * 4 + at.x) * 16
    four[at.y] = whole[pl.ds(pl.multiple_of(block, 16), 16), :]
    yield from spread(net, lambda p: four.at[p], at.y, along(at, "dy"))
    two[0] = sum_four(four)
    yield from swap(net, two.at[0], two.at[1], at.at(other=True))
    full[at.z, at.x] = two[0] + two[1]
    yield from spread(net, lambda p: full.at[p, at.x], at.z, along(at, "dz"))
    yield from spread(net, lambda p: full.at[:, p], at.x, along(at, "dx"))


def reduce_time(net, at, part, four_y, two_y, four_z, two_z, total):
    four_y[at.y] = part[...]
    yield from spread(net, lambda p: four_y.at[p], at.y, along(at, "dy"))
    two_y[0] = sum_four(four_y)
    yield from swap(net, two_y.at[0], two_y.at[1], at.at(other=True))
    four_z[at.z] = two_y[0] + two_y[1]
    yield from spread(net, lambda p: four_z.at[p], at.z, along(at, "dz"))
    two_z[0] = sum_four(four_z)
    yield from swap(net, two_z.at[0], two_z.at[1], at.at(dx=2))
    total[...] = two_z[0] + two_z[1]


def exact_dot(left, right):
    high = right.astype(BF16)
    rest = right - high.astype(F32)
    mid = rest.astype(BF16)
    low = (rest - mid.astype(F32)).astype(BF16)
    return (
        jnp.dot(left, low, preferred_element_type=F32)
        + jnp.dot(left, mid, preferred_element_type=F32)
        + jnp.dot(left, high, preferred_element_type=F32)
    )


def gram(ref):
    block = ref[...]
    return lax.dot_general(block, block, (((0,), (0,)), ((), ())), preferred_element_type=F32)


def gradient_kernel(
    coords, count, values, rows, cols, times, grad_a, grad_b, grad_c, s, plan, send, recv, local
):
    at = Place()
    net = Net(send, recv)
    a_full, b_full, c_full = s["a"], s["b"], s["c"]
    a_flat = a_full.reshape(16, EDGE, RANK)
    b_flat = b_full.reshape(16, EDGE, RANK)
    held, prefix = s["held"], s["prefix"]
    own = [
        pltpu.make_async_copy(cols.at[0], b_full.at[at.z, at.x], local.at[0]),
        pltpu.make_async_copy(rows.at[0], a_full.at[at.y, at.core, at.t], local.at[1]),
        pltpu.make_async_copy(times, c_full.at[at.t], local.at[2]),
        pltpu.make_async_copy(coords, s["coords"], local.at[3]),
    ]
    for copy in own:
        copy.start()
    part = SLOTS // LOADS
    loads = [
        pltpu.make_async_copy(
            values.at[part * i : part * i + part], held.at[part * i : part * i + part], local.at[4 + i]
        )
        for i in range(LOADS)
    ]
    for copy in loads:
        copy.start()
    at.greet()
    for copy in own:
        copy.wait()
    bring_b = gather_cols(net, at, b_full)
    bring_a = gather_rows(net, at, a_full)
    bring_c = swap(net, c_full.at[at.t], c_full.at[at.t], at.pair())
    next(bring_b)
    next(bring_a)
    next(bring_c)

    s["times"][0:32] = jnp.zeros((32, RANK), F32)
    s["times"][32:64] = c_full[at.t].astype(F32)
    prefix[0] = jnp.zeros((EDGE, RANK), F32)
    s["dots"][PADDED:LANES] = jnp.zeros((LANES - PADDED, RANK), F32)
    s["plan"][6:8] = jnp.zeros((2, LANES), jnp.int32)
    s["plan"][1:3] = jnp.zeros((2, LANES), jnp.int32)
    s["plan"][4:6] = jnp.zeros((2, LANES), jnp.int32)
    make_plan(s["plan"], s["coords"], count[0])
    tell = pltpu.make_async_copy(s["plan"], plan, local.at[4 + LOADS])
    tell.start()
    next(bring_b)
    next(bring_a)
    tell.wait()
    for copy in loads:
        copy.wait()
    drive(bring_b, bring_c)

    s["gram"][...] = gram(s["b"].reshape(16 * EDGE, RANK))
    share_b = gram_cols(net, at, s["gram"], s["gb4"], s["gb2"], s["gb"])
    next(share_b)
    next(bring_a)
    trips = PADDED // UNROLL
    tile_pass(plan, 0, (0, trips), held, s["times"], b_flat, False, prefix)

    def row_block(y, core, t):
        i = y * 4 + core * 2 + t
        return prefix[plan[2, i]] - prefix[plan[1, i]]

    part_a = reduce_rows(net, at, row_block, s["chip"], s["total_a"], s)
    next(part_a)
    drive(bring_a)
    next(share_b)
    s["gram"][...] = gram(s["a"].reshape(16 * EDGE, RANK))
    share_a = gram_rows(net, at, s["gram"], s["ga4"], s["ga2"], s["ga"])
    next(share_a)

    def more(first, last):
        tile_pass(
            plan, 3, (first, last), held, s["times"], a_flat, True, prefix, b_flat, s["dots"]
        )

    more(0, 5)
    next(part_a)
    next(share_b)
    next(share_a)
    more(5, trips)

    def col_block(z, x, h):
        i = z * 4 + x
        lanes = slice(128 * h, 128 * h + 128)
        return prefix[plan[5, i], :, lanes] - prefix[plan[4, i], :, lanes]

    def put(h):
        def total(value):
            s["total_b"][:, 128 * h : 128 * h + 128] = value

        return total

    part_b = [
        reduce_cols(
            net, at, lambda k, j: col_block((at.z + k) % 4, (at.x + j) % 4, 0),
            "dx", "dz", s["here0"], put(0), s["s10"], s["r10"], s["s20"], s["r20"],
        ),
        reduce_cols(
            net, at, lambda k, j: col_block((at.z + j) % 4, (at.x + k) % 4, 1),
            "dz", "dx", s["here1"], put(1), s["s11"], s["r11"], s["s21"], s["r21"],
        ),
    ]
    for run in part_b:
        next(run)
    snaps = s["plan"][3:4] >> 17
    pick = (snaps == iota((32, LANES), 0) + 32).astype(F32).astype(BF16)
    s["part_c"][...] = exact_dot(pick, s["dots"][...])
    part_c = reduce_time(
        net, at, s["part_c"], s["cy4"], s["cy2"], s["cz4"], s["cz2"], s["total_c"]
    )
    next(part_c)
    for _ in range(3):
        for run in part_b:
            next(run)
    drive(part_a, share_a, share_b, part_c, *part_b)

    whole_a = s["ga"][...].reshape(RANK, RANK)
    whole_b = s["gb"][...].reshape(RANK, RANK)
    whole_c = gram(c_full.reshape(64, RANK))
    grad_a[0] = exact_dot(a_full[at.y, at.core, at.t], whole_b * whole_c) - s["total_a"][...]
    grad_b[0] = exact_dot(b_full[at.z, at.x], whole_a * whole_c) - s["total_b"][...]
    grad_c[...] = exact_dot(c_full[at.t], whole_a * whole_b) - s["total_c"][...]
    net.close()


def hand_over(in_a, in_b, in_c, out_a, out_b, out_c, sems):
    made = [
        pltpu.make_async_copy(src, dst, sems.at[i])
        for i, (src, dst) in enumerate(((in_a, out_a), (in_b, out_b), (in_c, out_c)))
    ]
    for copy in made:
        copy.start()
    for copy in made:
        copy.wait()


def on_device(tile_values, tile_coords, tile_counts, factor_rows, factor_cols, factor_time):
    values = tile_values.reshape(SLOTS, EDGE, EDGE)
    coords = tile_coords.reshape(3, 1, SLOTS)
    count = tile_counts.reshape(1)
    wire = lambda *lead: pltpu.VMEM(lead + (RANK,), I16)
    half = lambda *lead: pltpu.VMEM(lead + (EDGE,), I16)
    real = lambda *lead: pltpu.VMEM(lead + (RANK,), F32)
    big = EDGE + PAD
    scratch = dict(
        a=pltpu.VMEM((4, 2, 2, EDGE, RANK), BF16),
        b=pltpu.VMEM((4, 4, EDGE, RANK), BF16),
        c=pltpu.VMEM((2, 32, RANK), BF16),
        held=pltpu.VMEM((SLOTS, EDGE, EDGE), BF16),
        prefix=real(ROUNDS + 1, EDGE),
        dots=real(LANES), times=real(64), part_c=real(32),
        plan=pltpu.VMEM((8, LANES), jnp.int32), coords=pltpu.VMEM((3, 1, SLOTS), jnp.int32),
        chip=real(4, 2, EDGE), total_a=real(EDGE), total_b=real(EDGE), total_c=real(32),
        core_s=wire(4, 2, big), core_r=wire(4, 2, big),
        y_s=wire(4, 2, big), y_r=wire(4, 2, big), x_s=wire(big), x_r=wire(big),
        s10=half(4, 4, big), r10=half(4, 4, big), s20=half(4, big), r20=half(4, big),
        s11=half(4, 4, big), r11=half(4, 4, big), s21=half(4, big), r21=half(4, big),
        here0=pltpu.VMEM((EDGE, EDGE), F32), here1=pltpu.VMEM((EDGE, EDGE), F32),
        gram=real(RANK),
        ga4=real(4, 16), ga2=real(2, 16), ga=real(4, 2, 2, 16),
        gb4=real(4, 16), gb2=real(2, 16), gb=real(4, 4, 16),
        cy4=real(4, 32), cy2=real(2, 32), cz4=real(4, 32), cz2=real(2, 32),
    )
    smem = pl.BlockSpec(memory_space=pltpu.SMEM)
    anywhere = pl.BlockSpec(memory_space=pl.ANY)
    whole = pl.BlockSpec(memory_space=pltpu.VMEM)
    shapes = (
        jax.ShapeDtypeStruct((1, EDGE, RANK), F32),
        jax.ShapeDtypeStruct((1, EDGE, RANK), F32),
        jax.ShapeDtypeStruct((32, RANK), F32),
    )
    copies = 128
    grads = pl.pallas_call(
        gradient_kernel,
        out_shape=shapes,
        in_specs=[anywhere, smem] + [anywhere] * 4,
        out_specs=(whole,) * 3,
        scratch_shapes=[
            scratch,
            pltpu.SMEM((8, LANES), jnp.int32),
            pltpu.SemaphoreType.DMA((copies,)),
            pltpu.SemaphoreType.DMA((copies,)),
            pltpu.SemaphoreType.DMA((5 + LOADS,)),
        ],
        compiler_params=pltpu.CompilerParams(
            collective_id=0, has_side_effects=True, vmem_limit_bytes=60 << 20
        ),
        name="gradient",
    )(coords, count, values, factor_rows, factor_cols, factor_time)
    return pl.pallas_call(
        hand_over,
        out_shape=shapes,
        in_specs=[anywhere] * 3,
        out_specs=(anywhere,) * 3,
        scratch_shapes=[pltpu.SemaphoreType.DMA((3,))],
        name="hand_over",
    )(*grads)


def solution(mesh):
    return jax.shard_map(
        on_device,
        mesh=mesh,
        in_specs=(
            P("row", "col", "tm", None, None, None),
            P("row", "col", "tm", None, None),
            P("row", "col", "tm"),
            P("row", ("col", "tm"), None),
            P("col", ("row", "tm"), None),
            P("tm", None),
        ),
        out_specs=(P("row", ("col", "tm"), None), P("col", ("row", "tm"), None), P("tm", None)),
        check_vma=False,
    )
```

time: 680 us -> 78.1 us (0.11)
  blocking collectives: 335 us -> 0 us
  matrix products: 135 us -> 0 us
  local copies, waits for them, and re-layouts: 103 us -> 0 us
  waiting for transfers between devices: 77.9 us -> 0 us
  Pallas kernels: 0 us -> 76.7 us
  between operations: 15.9 us -> 1.28 us
  other arithmetic: 11.3 us -> 0 us
    psum x1 -> x0, blocking collectives: 331 us -> none  [on_device(): mttkrp_time = lax.psum(sum_time, ('row', 'col'))]
    dot_general x54 -> x0, matrix products: 135 us -> none  [the longest x6 33.5 us: add_block(): jnp.einsum('na,nx->ax', row_hot.astype(jnp.float32), row_terms, precision...]
    while x48 -> x0, local copies, waits for them, and re-layouts: 89.3 us -> none
    pallas_call x0 -> x2, Pallas kernels: none -> 76.7 us  [the longest x1 66.6 us: on_device(): pl.pallas_call(gradient_kernel, out_shape=shapes, in_specs=[anywhere, sme...]
    all_gather x2 -> x0, waiting for transfers between devices: 76.5 us -> none  [the longest x1 45.2 us: on_device(): row_block = lax.all_gather(factor_rows, ('col', 'tm'), axis=1, tiled=True)]
    select_n x1 -> x0, other arithmetic: 10.6 us -> none  [on_device(): jnp.where(live_slots[:, None, None], tile_vals, jnp.zeros((), tile_vals.d...]
    reshape x4 -> x0, local copies, waits for them, and re-layouts: 7.96 us -> none  [the longest x2 4.41 us: on_device(): sum_rows = sum_rows.reshape(1, -1, rank_width)]
  transfers between devices with their start and end apart: 5 -> 0, of which waited for: 2 -> 0; matrix products, arithmetic and copies ran while one was open for 36% -> 0% of each run, Pallas kernels for 0% -> 0%
where the time goes in v2:
time: 78.1 us; the launch traced here: 78 us
  Pallas kernels  76.7 us (98%)
  between operations  1.28 us (2%)
    pallas_call x1, Pallas kernels, on_device(): pl.pallas_call(gradient_kernel, out_shape=shapes, in_specs=[anywhere, sme...  66.6 us
    pallas_call x1, Pallas kernels, on_device(): pl.pallas_call(hand_over, out_shape=shapes, in_specs=[anywhere] * 3, out_...  10.1 us

profile of v2, /device:TPU:0, one launch (start us, length us, event | category | flops | bytes accessed | tf_op | source)
XLA Modules:
  0.0 78.0 jit_solution(7180880089843246141)
XLA Ops:
  1.3 66.6 %gradient.1 = (f32[1,128,256]{2,1,0:T(8,128)}, f32[1,128,256]{2,1,0:T(8,128)}, f32[32,256]{1,0:T(8,128)}) custom-call(s32[3,1,384]{2,1,0:T(1,128)} %bitcast.5, s32[1]{0:T(128)} %bitcast.3.count, bf16[384,128,128]{2,1,0:T(8,128)(2,1)} %bitcast.4, bf16[1,128,256]{2,1,0:T(8,128)(2,1)} %rows.1, bf16[1,128,256]{2,1,0:T(8,128)(2,1)} %cols.1, bf16[32,256]{1,0:T(8,128)(2,1)} %times.1), custom_call_target="tpu_custom_call" | custom-call | tf_op jit(solution)/shard_map/gradient/pallas_call | solution.py:531
  67.9 10.1 %hand_over.1 = (f32[1,128,256]{2,1,0:T(8,128)}, f32[1,128,256]{2,1,0:T(8,128)}, f32[32,256]{1,0:T(8,128)}) custom-call(f32[1,128,256]{2,1,0:T(8,128)} %get-tuple-element.6.in_a, f32[1,128,256]{2,1,0:T(8,128)} %get-tuple-element.7.in_b, f32[32,256]{1,0:T(8,128)} %get-tuple-element.8.in_c), custom_call_target="tpu_custom_call" | custom-call | tf_op jit(solution)/shard_map/hand_over/pallas_call | solution.py:548

commit v3 on v2

--- a/solution.py
+++ b/solution.py
@@ -1,3 +1,5 @@
+from types import FunctionType
+
 import jax
 import jax.numpy as jnp
 from jax import lax
@@ -14,27 +16,42 @@
 PAD = 16
 
 
+class Copy:
+    def __init__(self, src, dst, send, recv, device):
+        self.src, self.dst, self.send, self.recv, self.device = src, dst, send, recv, device
+
+    def made(self):
+        return pltpu.make_async_remote_copy(
+            src_ref=self.src() if isinstance(self.src, FunctionType) else self.src,
+            dst_ref=self.dst() if isinstance(self.dst, FunctionType) else self.dst,
+            send_sem=self.send(),
+            recv_sem=self.recv(),
+            device_id=self.device,
+            device_id_type=MESH,
+        )
+
+    def wait_recv(self):
+        self.made().wait_recv()
+
+    def wait_send(self):
+        self.made().wait_send()
+
+
 class Net:
     def __init__(self, send, recv):
         self.send, self.recv, self.used, self.open = send, recv, 0, []
 
     def copy(self, src, dst, device):
-        made = pltpu.make_async_remote_copy(
-            src_ref=src,
-            dst_ref=dst,
-            send_sem=self.send.at[self.used],
-            recv_sem=self.recv.at[self.used],
-            device_id=device,
-            device_id_type=MESH,
-        )
+        n = self.used
+        copy = Copy(src, dst, lambda: self.send.at[n], lambda: self.recv.at[n], device)
         self.used += 1
-        made.start()
-        self.open.append(made)
-        return made
+        copy.made().start()
+        self.open.append(copy)
+        return copy
 
     def close(self):
-        for made in self.open:
-            made.wait_send()
+        for copy in self.open:
+            copy.wait_send()
 
 
 class Place:
@@ -42,23 +59,28 @@
         row, col, self.t = lax.axis_index("row"), lax.axis_index("col"), lax.axis_index("tm")
         self.z, self.y, self.core = row // 2, col // 2, col % 2
         self.x = (row % 2) * 2 + self.t
-
-    def at(self, dz=0, dy=0, dx=0, other=False):
-        z, y, x = (self.z + dz) % 4, (self.y + dy) % 4, (self.x + dx) % 4
-        core = 1 - self.core if other else self.core
-        return (z * 2 + x // 2, y * 2 + core, x % 2)
-
-    def pair(self):
-        return (self.z * 2 + self.x // 2, self.y * 2 + self.core, 1 - self.t)
+        self.far_t, self.far_core = 1 - self.t, 1 - self.core
+        self.zs = [self.z] + [(self.z + k) % 4 for k in (1, 2, 3)]
+        self.ys = [self.y] + [(self.y + k) % 4 for k in (1, 2, 3)]
+        self.xs = [self.x] + [(self.x + k) % 4 for k in (1, 2, 3)]
+        mine = (row, col, self.t)
+        self.dz = [mine] + [(z * 2 + self.x // 2, col, self.t) for z in self.zs[1:]]
+        self.dy = [mine] + [(row, y * 2 + self.core, self.t) for y in self.ys[1:]]
+        self.dx = [mine] + [(self.z * 2 + x // 2, col, x % 2) for x in self.xs[1:]]
+        self.other = (row, self.y * 2 + self.far_core, self.t)
+        self.pair = (row, col, self.far_t)
 
     def greet(self):
         barrier = pltpu.get_barrier_semaphore()
-        others = [self.at(other=True)]
-        for step in (1, 2, 3):
-            others += [self.at(dz=step), self.at(dy=step), self.at(dx=step)]
+        others = [self.other] + self.dz[1:] + self.dy[1:] + self.dx[1:]
         for device in others:
             pl.semaphore_signal(barrier, inc=1, device_id=device, device_id_type=MESH)
         pl.semaphore_wait(barrier, len(others))
+
+
+def step(run, *more):
+    for each in (run,) + more:
+        next(each, None)
 
 
 def drive(*runs):
@@ -70,7 +92,7 @@
 
 
 def spread(net, view, me, devices):
-    made = [net.copy(view(me), view(me), device) for device in devices]
+    made = [net.copy(lambda: view(me), lambda: view(me), device) for device in devices]
     yield 1
     for copy in made:
         copy.wait_recv()
@@ -161,28 +183,28 @@
     plan_groups(plan, 3, cols, (tall >> 13) & 15, tall)
 
 
-def gather_rows(net, at, full):
+def gather_rows(net, at, full, source):
     own = full.at[at.y, at.core, at.t]
-    pair = net.copy(own, own, at.pair())
-    mine = [net.copy(own, own, at.at(dy=k)) for k in (1, 3, 2)]
+    pair = net.copy(source, own, at.pair)
+    mine = [net.copy(source, own, at.dy[k]) for k in (1, 3, 2)]
     yield 1
     pair.wait_recv()
-    other = full.at[at.y, at.core, 1 - at.t]
-    far = [net.copy(other, other, at.at(dy=k)) for k in (1, 3, 2)]
+    other = full.at[at.y, at.core, at.far_t]
+    far = [net.copy(other, other, at.dy[k]) for k in (1, 3, 2)]
     near = full.at[at.y, at.core]
-    across = [net.copy(near, near, at.at(other=True))]
+    across = [net.copy(near, near, at.other)]
     yield 1
     for k, first, second in zip((1, 3, 2), mine, far):
         first.wait_recv()
         second.wait_recv()
-        came = full.at[(at.y + 4 - k) % 4, at.core]
-        across.append(net.copy(came, came, at.at(other=True)))
+        came = full.at[at.ys[4 - k], at.core]
+        across.append(net.copy(came, came, at.other))
     yield 1
     for copy in across:
         copy.wait_recv()
 
 
-def gather_cols(net, at, full):
+def gather_cols(net, at, full, source):
     def low(z):
         return full.at[z, at.x, 0:64]
 
@@ -190,31 +212,34 @@
         return full.at[at.z, x, 64:128]
 
     order = (1, 3, 2)
-    low_in = [net.copy(low(at.z), low(at.z), at.at(dz=k)) for k in order]
-    high_in = [net.copy(high(at.x), high(at.x), at.at(dx=k)) for k in order]
+    own_low, own_high = source.at[0:64], source.at[64:128]
+    low_in = [net.copy(own_low, low(at.z), at.dz[k]) for k in order]
+    high_in = [net.copy(own_high, high(at.x), at.dx[k]) for k in order]
     rest = []
     for k in order:
-        rest.append(net.copy(low(at.z), low(at.z), at.at(dx=k)))
-        rest.append(net.copy(high(at.x), high(at.x), at.at(dz=k)))
+        rest.append(net.copy(own_low, low(at.z), at.dx[k]))
+        rest.append(net.copy(own_high, high(at.x), at.dz[k]))
     yield 1
     for k, from_z, from_x in zip(order, low_in, high_in):
         from_z.wait_recv()
-        came = low((at.z + 4 - k) % 4)
-        rest += [net.copy(came, came, at.at(dx=j)) for j in order]
+        came = low(at.zs[4 - k])
+        rest += [net.copy(came, came, at.dx[j]) for j in order]
         from_x.wait_recv()
-        came = high((at.x + 4 - k) % 4)
-        rest += [net.copy(came, came, at.at(dz=j)) for j in order]
+        came = high(at.xs[4 - k])
+        rest += [net.copy(came, came, at.dz[j]) for j in order]
     yield 1
     for copy in rest:
         copy.wait_recv()
 
 
-def tile_pass(plan, line, trips, held, times, operand, turned, prefix, other=None, dots=None):
+def tile_pass(plan, line, held, times, operand, turned, prefix, hooks, other=None, dots=None):
     key = 13 if line == 0 else 9
     back = 9 if line == 0 else 13
 
-    @pl.loop(*trips)
+    @pl.loop(0, PADDED // UNROLL)
     def _(trip):
+        for when, hook in hooks.items():
+            pl.when(trip == when)(hook)
         total = prefix[trip * (UNROLL // ROUND)]
         for j in range(UNROLL // ROUND):
             for u in range(ROUND):
@@ -232,18 +257,20 @@
             prefix[trip * (UNROLL // ROUND) + j + 1] = total
 
 
+def at_step(ref, k):
+    return lambda: ref.at[k]
+
+
 def reduce_rows(net, at, block, chip, total, s):
     order = (2, 1, 3, 0)
     made = {}
     for k in order:
-        y = (at.y + k) % 4
         for h in range(2):
-            encode(s["core_s"].at[k, h], block(y, 1 - at.core, h))
-        made[k] = net.copy(s["core_s"].at[k], s["core_r"].at[k], at.at(other=True))
+            encode(s["core_s"].at[k, h], block(at.ys[k], at.far_core, h))
+        made[k] = net.copy(at_step(s["core_s"], k), at_step(s["core_r"], k), at.other)
     for k in order:
-        y = (at.y + k) % 4
         for h in range(2):
-            chip[k, h] = block(y, at.core, h)
+            chip[k, h] = block(at.ys[k], at.core, h)
     yield 1
     sent = {}
     for k in order:
@@ -255,24 +282,24 @@
             else:
                 chip[0, h] = value
         if k:
-            sent[k] = net.copy(s["y_s"].at[k], s["y_r"].at[k], at.at(dy=k))
+            sent[k] = net.copy(at_step(s["y_s"], k), at_step(s["y_r"], k), at.dy[k])
     yield 1
     for k in (1, 3, 2):
         sent[k].wait_recv()
         for h in range(2):
             chip[0, h] += decode(s["y_r"].at[k, h])
-    encode(s["x_s"], chip[0, 1 - at.t])
-    yield from swap(net, s["x_s"], s["x_r"], at.pair())
+    encode(s["x_s"], chip[0, at.far_t])
+    yield from swap(net, s["x_s"], s["x_r"], at.pair)
     total[...] = chip[0, at.t] + decode(s["x_r"])
 
 
-def reduce_cols(net, at, block, first, second, here, total, s1, r1, s2, r2):
+def reduce_cols(net, block, first, second, here, total, s1, r1, s2, r2):
     order = (2, 1, 3, 0)
     made = {}
     for k in order:
         for j in (2, 1, 3):
             encode(s1.at[k, j], block(k, j))
-            made[k, j] = net.copy(s1.at[k, j], r1.at[k, j], at.at(**{first: j}))
+            made[k, j] = net.copy(s1.at[k, j], r1.at[k, j], first[j])
         yield 1
     sent = {}
     for k in order:
@@ -283,7 +310,7 @@
             value = value + decode(r1.at[k, j])
         if k:
             encode(s2.at[k], value)
-            sent[k] = net.copy(s2.at[k], r2.at[k], at.at(**{second: k}))
+            sent[k] = net.copy(s2.at[k], r2.at[k], second[k])
         else:
             here[...] = value
         yield 1
@@ -294,10 +321,6 @@
     total(value)
 
 
-def along(at, name):
-    return [at.at(**{name: step}) for step in (1, 2, 3)]
-
-
 def sum_four(ref):
     return (ref[0] + ref[1]) + (ref[2] + ref[3])
 
@@ -305,35 +328,35 @@
 def gram_rows(net, at, whole, four, two, full):
     block = (at.y * 4 + at.core * 2 + at.t) * 16
     four[at.z] = whole[pl.ds(pl.multiple_of(block, 16), 16), :]
-    yield from spread(net, lambda p: four.at[p], at.z, along(at, "dz"))
+    yield from spread(net, lambda p: four.at[p], at.z, at.dz[1:])
     two[0] = sum_four(four)
-    yield from swap(net, two.at[0], two.at[1], at.at(dx=2))
+    yield from swap(net, at_step(two, 0), at_step(two, 1), at.dx[2])
     full[at.y, at.core, at.t] = two[0] + two[1]
-    yield from swap(net, full.at[at.y, at.core, at.t], full.at[at.y, at.core, at.t], at.pair())
-    yield from spread(net, lambda p: full.at[p, at.core], at.y, along(at, "dy"))
-    yield from swap(net, full.at[:, at.core], full.at[:, at.core], at.at(other=True))
+    yield from swap(net, lambda: full.at[at.y, at.core, at.t], lambda: full.at[at.y, at.core, at.t], at.pair)
+    yield from spread(net, lambda p: full.at[p, at.core], at.y, at.dy[1:])
+    yield from swap(net, lambda: full.at[:, at.core], lambda: full.at[:, at.core], at.other)
 
 
 def gram_cols(net, at, whole, four, two, full):
     block = (at.z * 4 + at.x) * 16
     four[at.y] = whole[pl.ds(pl.multiple_of(block, 16), 16), :]
-    yield from spread(net, lambda p: four.at[p], at.y, along(at, "dy"))
+    yield from spread(net, lambda p: four.at[p], at.y, at.dy[1:])
     two[0] = sum_four(four)
-    yield from swap(net, two.at[0], two.at[1], at.at(other=True))
+    yield from swap(net, at_step(two, 0), at_step(two, 1), at.other)
     full[at.z, at.x] = two[0] + two[1]
-    yield from spread(net, lambda p: full.at[p, at.x], at.z, along(at, "dz"))
-    yield from spread(net, lambda p: full.at[:, p], at.x, along(at, "dx"))
+    yield from spread(net, lambda p: full.at[p, at.x], at.z, at.dz[1:])
+    yield from spread(net, lambda p: full.at[:, p], at.x, at.dx[1:])
 
 
 def reduce_time(net, at, part, four_y, two_y, four_z, two_z, total):
     four_y[at.y] = part[...]
-    yield from spread(net, lambda p: four_y.at[p], at.y, along(at, "dy"))
+    yield from spread(net, lambda p: four_y.at[p], at.y, at.dy[1:])
     two_y[0] = sum_four(four_y)
-    yield from swap(net, two_y.at[0], two_y.at[1], at.at(other=True))
+    yield from swap(net, at_step(two_y, 0), at_step(two_y, 1), at.other)
     four_z[at.z] = two_y[0] + two_y[1]
-    yield from spread(net, lambda p: four_z.at[p], at.z, along(at, "dz"))
+    yield from spread(net, lambda p: four_z.at[p], at.z, at.dz[1:])
     two_z[0] = sum_four(four_z)
-    yield from swap(net, two_z.at[0], two_z.at[1], at.at(dx=2))
+    yield from swap(net, at_step(two_z, 0), at_step(two_z, 1), at.dx[2])
     total[...] = two_z[0] + two_z[1]
 
 
@@ -381,114 +404,124 @@
     for copy in loads:
         copy.start()
     at.greet()
+    bring_b = gather_cols(net, at, b_full, cols.at[0])
+    bring_a = gather_rows(net, at, a_full, rows.at[0])
+    bring_c = swap(net, times, c_full.at[at.t], at.pair)
+    step(bring_b, bring_a, bring_c)
     for copy in own:
         copy.wait()
-    bring_b = gather_cols(net, at, b_full)
-    bring_a = gather_rows(net, at, a_full)
-    bring_c = swap(net, c_full.at[at.t], c_full.at[at.t], at.pair())
-    next(bring_b)
-    next(bring_a)
-    next(bring_c)
 
     s["times"][0:32] = jnp.zeros((32, RANK), F32)
     s["times"][32:64] = c_full[at.t].astype(F32)
     prefix[0] = jnp.zeros((EDGE, RANK), F32)
     s["dots"][PADDED:LANES] = jnp.zeros((LANES - PADDED, RANK), F32)
-    s["plan"][6:8] = jnp.zeros((2, LANES), jnp.int32)
-    s["plan"][1:3] = jnp.zeros((2, LANES), jnp.int32)
-    s["plan"][4:6] = jnp.zeros((2, LANES), jnp.int32)
+    for line in (1, 4, 6):
+        s["plan"][line : line + 2] = jnp.zeros((2, LANES), jnp.int32)
     make_plan(s["plan"], s["coords"], count[0])
     tell = pltpu.make_async_copy(s["plan"], plan, local.at[4 + LOADS])
     tell.start()
-    next(bring_b)
-    next(bring_a)
+    step(bring_b, bring_a)
     tell.wait()
     for copy in loads:
         copy.wait()
-    drive(bring_b, bring_c)
-
-    s["gram"][...] = gram(s["b"].reshape(16 * EDGE, RANK))
+    step(bring_a)
+    drive(bring_b, bring_a, bring_c)
+
+    s["gram"][...] = gram(b_full.reshape(16 * EDGE, RANK))
     share_b = gram_cols(net, at, s["gram"], s["gb4"], s["gb2"], s["gb"])
-    next(share_b)
-    next(bring_a)
-    trips = PADDED // UNROLL
-    tile_pass(plan, 0, (0, trips), held, s["times"], b_flat, False, prefix)
+    share_a = gram_rows(net, at, s["gram_a"], s["ga4"], s["ga2"], s["ga"])
+    step(share_b)
+
+    def start_a():
+        s["gram_a"][...] = gram(a_full.reshape(16 * EDGE, RANK))
+        step(share_a)
+
+    hooks = {
+        2: start_a,
+        4: lambda: step(share_b),
+        5: lambda: step(share_a),
+        7: lambda: step(share_b),
+        8: lambda: step(share_a),
+    }
+    tile_pass(
+        plan, 0, held, s["times"], b_flat, False, prefix, hooks, a_flat, s["dots"]
+    )
 
     def row_block(y, core, t):
         i = y * 4 + core * 2 + t
         return prefix[plan[2, i]] - prefix[plan[1, i]]
 
     part_a = reduce_rows(net, at, row_block, s["chip"], s["total_a"], s)
-    next(part_a)
-    drive(bring_a)
-    next(share_b)
-    s["gram"][...] = gram(s["a"].reshape(16 * EDGE, RANK))
-    share_a = gram_rows(net, at, s["gram"], s["ga4"], s["ga2"], s["ga"])
-    next(share_a)
-
-    def more(first, last):
-        tile_pass(
-            plan, 3, (first, last), held, s["times"], a_flat, True, prefix, b_flat, s["dots"]
-        )
-
-    more(0, 5)
-    next(part_a)
-    next(share_b)
-    next(share_a)
-    more(5, trips)
-
-    def col_block(z, x, h):
-        i = z * 4 + x
-        lanes = slice(128 * h, 128 * h + 128)
-        return prefix[plan[5, i], :, lanes] - prefix[plan[4, i], :, lanes]
-
-    def put(h):
-        def total(value):
-            s["total_b"][:, 128 * h : 128 * h + 128] = value
-
-        return total
-
-    part_b = [
-        reduce_cols(
-            net, at, lambda k, j: col_block((at.z + k) % 4, (at.x + j) % 4, 0),
-            "dx", "dz", s["here0"], put(0), s["s10"], s["r10"], s["s20"], s["r20"],
-        ),
-        reduce_cols(
-            net, at, lambda k, j: col_block((at.z + j) % 4, (at.x + k) % 4, 1),
-            "dz", "dx", s["here1"], put(1), s["s11"], s["r11"], s["s21"], s["r21"],
-        ),
-    ]
-    for run in part_b:
-        next(run)
-    snaps = s["plan"][3:4] >> 17
+    step(part_a)
+    snaps = s["plan"][0:1] >> 17
     pick = (snaps == iota((32, LANES), 0) + 32).astype(F32).astype(BF16)
     s["part_c"][...] = exact_dot(pick, s["dots"][...])
     part_c = reduce_time(
         net, at, s["part_c"], s["cy4"], s["cy2"], s["cz4"], s["cz2"], s["total_c"]
     )
-    next(part_c)
-    for _ in range(3):
-        for run in part_b:
-            next(run)
-    drive(part_a, share_a, share_b, part_c, *part_b)
-
+    step(part_c)
+    hooks = {
+        1: lambda: step(share_b),
+        2: lambda: step(share_a),
+        3: lambda: step(part_a, part_c),
+        5: lambda: step(share_b, share_a),
+        6: lambda: step(part_c),
+        8: lambda: step(share_a),
+        9: lambda: step(part_c),
+    }
+    tile_pass(plan, 3, held, s["times"], a_flat, True, prefix, hooks)
+
+    def col_block(z, x, h):
+        i = z * 4 + x
+        lanes = slice(128 * h, 128 * h + 128)
+        return prefix[plan[5, i], :, lanes] - prefix[plan[4, i], :, lanes]
+
+    def put(h):
+        def total(value):
+            s["total_b"][:, 128 * h : 128 * h + 128] = value
+
+        return total
+
+    part_b = [
+        reduce_cols(
+            net, lambda k, j: col_block(at.zs[k], at.xs[j], 0),
+            at.dx, at.dz, s["here0"], put(0), s["s10"], s["r10"], s["s20"], s["r20"],
+        ),
+        reduce_cols(
+            net, lambda k, j: col_block(at.zs[j], at.xs[k], 1),
+            at.dz, at.dx, s["here1"], put(1), s["s11"], s["r11"], s["s21"], s["r21"],
+        ),
+    ]
+    for _ in range(4):
+        step(*part_b)
+    step(part_a)
+    step(*part_b)
+    step(part_c)
     whole_a = s["ga"][...].reshape(RANK, RANK)
     whole_b = s["gb"][...].reshape(RANK, RANK)
     whole_c = gram(c_full.reshape(64, RANK))
-    grad_a[0] = exact_dot(a_full[at.y, at.core, at.t], whole_b * whole_c) - s["total_a"][...]
-    grad_b[0] = exact_dot(b_full[at.z, at.x], whole_a * whole_c) - s["total_b"][...]
     grad_c[...] = exact_dot(c_full[at.t], whole_a * whole_b) - s["total_c"][...]
+    s["near_a"][...] = exact_dot(a_full[at.y, at.core, at.t], whole_b * whole_c)
+    step(*part_b)
+    s["near_b"][...] = exact_dot(b_full[at.z, at.x], whole_a * whole_c)
+    step(*part_b)
+    step(part_a)
+    grad_a[0] = s["near_a"][...] - s["total_a"][...]
+    drive(*part_b)
+    grad_b[0] = s["near_b"][...] - s["total_b"][...]
     net.close()
 
 
-def hand_over(in_a, in_b, in_c, out_a, out_b, out_c, sems):
-    made = [
-        pltpu.make_async_copy(src, dst, sems.at[i])
-        for i, (src, dst) in enumerate(((in_a, out_a), (in_b, out_b), (in_c, out_c)))
-    ]
-    for copy in made:
+def hand_over(in_a, in_b, in_c, out_a, out_b, out_c, held_a, held_b, held_c, sems):
+    path = ((in_a, held_a, out_a), (in_b, held_b, out_b), (in_c, held_c, out_c))
+    bring = [pltpu.make_async_copy(p[0], p[1], sems.at[i]) for i, p in enumerate(path)]
+    leave = [pltpu.make_async_copy(p[1], p[2], sems.at[3 + i]) for i, p in enumerate(path)]
+    for copy in bring:
         copy.start()
-    for copy in made:
+    for came, gone in zip(bring, leave):
+        came.wait()
+        gone.start()
+    for copy in leave:
         copy.wait()
 
 
@@ -514,7 +547,7 @@
         s10=half(4, 4, big), r10=half(4, 4, big), s20=half(4, big), r20=half(4, big),
         s11=half(4, 4, big), r11=half(4, 4, big), s21=half(4, big), r21=half(4, big),
         here0=pltpu.VMEM((EDGE, EDGE), F32), here1=pltpu.VMEM((EDGE, EDGE), F32),
-        gram=real(RANK),
+        gram=real(RANK), gram_a=real(RANK), near_a=real(EDGE), near_b=real(EDGE),
         ga4=real(4, 16), ga2=real(2, 16), ga=real(4, 2, 2, 16),
         gb4=real(4, 16), gb2=real(2, 16), gb=real(4, 4, 16),
         cy4=real(4, 32), cy2=real(2, 32), cz4=real(4, 32), cz2=real(2, 32),
@@ -550,7 +583,9 @@
         out_shape=shapes,
         in_specs=[anywhere] * 3,
         out_specs=(anywhere,) * 3,
-        scratch_shapes=[pltpu.SemaphoreType.DMA((3,))],
+        scratch_shapes=[pltpu.VMEM(kind.shape, F32) for kind in shapes]
+        + [pltpu.SemaphoreType.DMA((6,))],
+        compiler_params=pltpu.CompilerParams(vmem_limit_bytes=60 << 20),
         name="hand_over",
     )(*grads)
 

time: 78.1 us -> 65.8 us (0.84)
  Pallas kernels: 76.7 us -> 64.1 us
    pallas_call x1, Pallas kernels: 10.1 us -> 1.68 us  [on_device(): pl.pallas_call(hand_over, out_shape=shapes, in_specs=[anywhere] * 3, out_...]
    pallas_call x1, Pallas kernels: 66.6 us -> 62.4 us  [on_device(): pl.pallas_call(gradient_kernel, out_shape=shapes, in_specs=[anywhere, sme...]
where the time goes in v3:
time: 65.8 us; the launch traced here: 65.4 us
  Pallas kernels  64.1 us (97%)
  between operations  1.28 us (2%)
    pallas_call x1, Pallas kernels, on_device(): pl.pallas_call(gradient_kernel, out_shape=shapes, in_specs=[anywhere, sme...  62.4 us
    pallas_call x1, Pallas kernels, on_device(): pl.pallas_call(hand_over, out_shape=shapes, in_specs=[anywhere] * 3, out_...  1.68 us

profile of v3, /device:TPU:0, one launch (start us, length us, event | category | flops | bytes accessed | tf_op | source)
XLA Modules:
  0.0 65.4 jit_solution(977492768485361287)
XLA Ops:
  1.3 62.4 %gradient.1 = (f32[1,128,256]{2,1,0:T(8,128)}, f32[1,128,256]{2,1,0:T(8,128)}, f32[32,256]{1,0:T(8,128)}) custom-call(s32[3,1,384]{2,1,0:T(1,128)} %bitcast.5, s32[1]{0:T(128)} %bitcast.3.count, bf16[384,128,128]{2,1,0:T(8,128)(2,1)} %bitcast.4, bf16[1,128,256]{2,1,0:T(8,128)(2,1)} %rows.1, bf16[1,128,256]{2,1,0:T(8,128)(2,1)} %cols.1, bf16[32,256]{1,0:T(8,128)(2,1)} %times.1), custom_call_target="tpu_custom_call" | custom-call | tf_op jit(solution)/shard_map/gradient/pallas_call | solution.py:564
  63.7 1.7 %hand_over.1 = (f32[1,128,256]{2,1,0:T(8,128)}, f32[1,128,256]{2,1,0:T(8,128)}, f32[32,256]{1,0:T(8,128)}) custom-call(f32[1,128,256]{2,1,0:T(8,128)} %get-tuple-element.6.in_a, f32[1,128,256]{2,1,0:T(8,128)} %get-tuple-element.7.in_b, f32[32,256]{1,0:T(8,128)} %get-tuple-element.8.in_c), custom_call_target="tpu_custom_call" | custom-call | tf_op jit(solution)/shard_map/hand_over/pallas_call | solution.py:581

commit v4 on v3

--- a/solution.py
+++ b/solution.py
@@ -186,17 +186,17 @@
 def gather_rows(net, at, full, source):
     own = full.at[at.y, at.core, at.t]
     pair = net.copy(source, own, at.pair)
-    mine = [net.copy(source, own, at.dy[k]) for k in (1, 3, 2)]
+    mine = {k: net.copy(source, own, at.dy[k]) for k in (2, 1, 3)}
     yield 1
     pair.wait_recv()
     other = full.at[at.y, at.core, at.far_t]
-    far = [net.copy(other, other, at.dy[k]) for k in (1, 3, 2)]
+    far = {k: net.copy(other, other, at.dy[k]) for k in (2, 1, 3)}
     near = full.at[at.y, at.core]
     across = [net.copy(near, near, at.other)]
     yield 1
-    for k, first, second in zip((1, 3, 2), mine, far):
-        first.wait_recv()
-        second.wait_recv()
+    for k in (1, 3, 2):
+        mine[k].wait_recv()
+        far[k].wait_recv()
         came = full.at[at.ys[4 - k], at.core]
         across.append(net.copy(came, came, at.other))
     yield 1
@@ -211,20 +211,21 @@
     def high(x):
         return full.at[at.z, x, 64:128]
 
-    order = (1, 3, 2)
+    order = (2, 1, 3)
     own_low, own_high = source.at[0:64], source.at[64:128]
-    low_in = [net.copy(own_low, low(at.z), at.dz[k]) for k in order]
-    high_in = [net.copy(own_high, high(at.x), at.dx[k]) for k in order]
-    rest = []
+    low_in, high_in, rest = {}, {}, []
+    for k in order:
+        low_in[k] = net.copy(own_low, low(at.z), at.dz[k])
+        high_in[k] = net.copy(own_high, high(at.x), at.dx[k])
     for k in order:
         rest.append(net.copy(own_low, low(at.z), at.dx[k]))
         rest.append(net.copy(own_high, high(at.x), at.dz[k]))
     yield 1
-    for k, from_z, from_x in zip(order, low_in, high_in):
-        from_z.wait_recv()
+    for k in (1, 3, 2):
+        low_in[k].wait_recv()
         came = low(at.zs[4 - k])
         rest += [net.copy(came, came, at.dx[j]) for j in order]
-        from_x.wait_recv()
+        high_in[k].wait_recv()
         came = high(at.xs[4 - k])
         rest += [net.copy(came, came, at.dz[j]) for j in order]
     yield 1
@@ -401,13 +402,13 @@
         )
         for i in range(LOADS)
     ]
-    for copy in loads:
-        copy.start()
     at.greet()
     bring_b = gather_cols(net, at, b_full, cols.at[0])
     bring_a = gather_rows(net, at, a_full, rows.at[0])
     bring_c = swap(net, times, c_full.at[at.t], at.pair)
-    step(bring_b, bring_a, bring_c)
+    step(bring_a, bring_b, bring_c)
+    for copy in loads:
+        copy.start()
     for copy in own:
         copy.wait()
 
@@ -420,7 +421,7 @@
     make_plan(s["plan"], s["coords"], count[0])
     tell = pltpu.make_async_copy(s["plan"], plan, local.at[4 + LOADS])
     tell.start()
-    step(bring_b, bring_a)
+    step(bring_a, bring_b)
     tell.wait()
     for copy in loads:
         copy.wait()
@@ -429,20 +430,11 @@
 
     s["gram"][...] = gram(b_full.reshape(16 * EDGE, RANK))
     share_b = gram_cols(net, at, s["gram"], s["gb4"], s["gb2"], s["gb"])
+    step(share_b)
+    s["gram_a"][...] = gram(a_full.reshape(16 * EDGE, RANK))
     share_a = gram_rows(net, at, s["gram_a"], s["ga4"], s["ga2"], s["ga"])
-    step(share_b)
-
-    def start_a():
-        s["gram_a"][...] = gram(a_full.reshape(16 * EDGE, RANK))
-        step(share_a)
-
-    hooks = {
-        2: start_a,
-        4: lambda: step(share_b),
-        5: lambda: step(share_a),
-        7: lambda: step(share_b),
-        8: lambda: step(share_a),
-    }
+    step(share_a)
+    hooks = {5: lambda: step(share_b, share_a), 7: lambda: step(share_b)}
     tile_pass(
         plan, 0, held, s["times"], b_flat, False, prefix, hooks, a_flat, s["dots"]
     )
@@ -461,13 +453,12 @@
     )
     step(part_c)
     hooks = {
-        1: lambda: step(share_b),
-        2: lambda: step(share_a),
-        3: lambda: step(part_a, part_c),
-        5: lambda: step(share_b, share_a),
-        6: lambda: step(part_c),
-        8: lambda: step(share_a),
-        9: lambda: step(part_c),
+        1: lambda: step(share_a),
+        2: lambda: step(share_b),
+        4: lambda: step(part_a, share_a),
+        5: lambda: step(part_c),
+        7: lambda: step(part_c),
+        9: lambda: step(share_b, share_a),
     }
     tile_pass(plan, 3, held, s["times"], a_flat, True, prefix, hooks)
 
@@ -494,16 +485,18 @@
     ]
     for _ in range(4):
         step(*part_b)
-    step(part_a)
-    step(*part_b)
-    step(part_c)
+    step(share_a, part_c)
     whole_a = s["ga"][...].reshape(RANK, RANK)
     whole_b = s["gb"][...].reshape(RANK, RANK)
     whole_c = gram(c_full.reshape(64, RANK))
+    s["near_a"][...] = exact_dot(a_full[at.y, at.core, at.t], whole_b * whole_c)
+    s["near_b"][...] = exact_dot(b_full[at.z, at.x], whole_a * whole_c)
+    step(*part_b)
+    step(part_a)
+    step(*part_b)
+    step(*part_b)
+    step(part_c)
     grad_c[...] = exact_dot(c_full[at.t], whole_a * whole_b) - s["total_c"][...]
-    s["near_a"][...] = exact_dot(a_full[at.y, at.core, at.t], whole_b * whole_c)
-    step(*part_b)
-    s["near_b"][...] = exact_dot(b_full[at.z, at.x], whole_a * whole_c)
     step(*part_b)
     step(part_a)
     grad_a[0] = s["near_a"][...] - s["total_a"][...]

time: 65.8 us -> 64.2 us (0.976)
  Pallas kernels: 64.1 us -> 62.8 us
    pallas_call x1, Pallas kernels: 62.4 us -> 61.1 us  [on_device(): pl.pallas_call(gradient_kernel, out_shape=shapes, in_specs=[anywhere, sme...]
where the time goes in v4:
time: 64.2 us; the launch traced here: 64 us
  Pallas kernels  62.8 us (98%)
  between operations  1.28 us (2%)
    pallas_call x1, Pallas kernels, on_device(): pl.pallas_call(gradient_kernel, out_shape=shapes, in_specs=[anywhere, sme...  61.1 us
    pallas_call x1, Pallas kernels, on_device(): pl.pallas_call(hand_over, out_shape=shapes, in_specs=[anywhere] * 3, out_...  1.68 us

profile of v4, /device:TPU:0, one launch (start us, length us, event | category | flops | bytes accessed | tf_op | source)
XLA Modules:
  0.0 64.0 jit_solution(2893153979157691595)
XLA Ops:
  1.3 61.1 %gradient.1 = (f32[1,128,256]{2,1,0:T(8,128)}, f32[1,128,256]{2,1,0:T(8,128)}, f32[32,256]{1,0:T(8,128)}) custom-call(s32[3,1,384]{2,1,0:T(1,128)} %bitcast.5, s32[1]{0:T(128)} %bitcast.3.count, bf16[384,128,128]{2,1,0:T(8,128)(2,1)} %bitcast.4, bf16[1,128,256]{2,1,0:T(8,128)(2,1)} %rows.1, bf16[1,128,256]{2,1,0:T(8,128)(2,1)} %cols.1, bf16[32,256]{1,0:T(8,128)(2,1)} %times.1), custom_call_target="tpu_custom_call" | custom-call | tf_op jit(solution)/shard_map/gradient/pallas_call | solution.py:557
  62.4 1.7 %hand_over.1 = (f32[1,128,256]{2,1,0:T(8,128)}, f32[1,128,256]{2,1,0:T(8,128)}, f32[32,256]{1,0:T(8,128)}) custom-call(f32[1,128,256]{2,1,0:T(8,128)} %get-tuple-element.6.in_a, f32[1,128,256]{2,1,0:T(8,128)} %get-tuple-element.7.in_b, f32[32,256]{1,0:T(8,128)} %get-tuple-element.8.in_c), custom_call_target="tpu_custom_call" | custom-call | tf_op jit(solution)/shard_map/hand_over/pallas_call | solution.py:574

commit v5 on v4

--- a/solution.py
+++ b/solution.py
@@ -273,25 +273,27 @@
         for h in range(2):
             chip[k, h] = block(at.ys[k], at.core, h)
     yield 1
-    sent = {}
+    paired = {}
     for k in order:
         made[k].wait_recv()
         for h in range(2):
-            value = chip[k, h] + decode(s["core_r"].at[k, h])
-            if k:
-                encode(s["y_s"].at[k, h], value)
-            else:
-                chip[0, h] = value
+            chip[k, h] += decode(s["core_r"].at[k, h])
+        encode(s["x_s"].at[k], chip[k, at.far_t])
+        paired[k] = net.copy(at_step(s["x_s"], k), at_step(s["x_r"], k), at.pair)
+    yield 1
+    sent = {}
+    for k in order:
+        paired[k].wait_recv()
+        value = chip[k, at.t] + decode(s["x_r"].at[k])
         if k:
+            encode(s["y_s"].at[k], value)
             sent[k] = net.copy(at_step(s["y_s"], k), at_step(s["y_r"], k), at.dy[k])
+        else:
+            total[...] = value
     yield 1
     for k in (1, 3, 2):
         sent[k].wait_recv()
-        for h in range(2):
-            chip[0, h] += decode(s["y_r"].at[k, h])
-    encode(s["x_s"], chip[0, at.far_t])
-    yield from swap(net, s["x_s"], s["x_r"], at.pair)
-    total[...] = chip[0, at.t] + decode(s["x_r"])
+        total[...] += decode(s["y_r"].at[k])
 
 
 def reduce_cols(net, block, first, second, here, total, s1, r1, s2, r2):
@@ -349,16 +351,16 @@
     yield from spread(net, lambda p: full.at[:, p], at.x, at.dx[1:])
 
 
-def reduce_time(net, at, part, four_y, two_y, four_z, two_z, total):
-    four_y[at.y] = part[...]
+def reduce_time(net, at, part, two_x, four_z, two_c, four_y, total):
+    two_x[0] = part[...]
+    yield from swap(net, at_step(two_x, 0), at_step(two_x, 1), at.dx[2])
+    four_z[at.z] = two_x[0] + two_x[1]
+    yield from spread(net, lambda p: four_z.at[p], at.z, at.dz[1:])
+    two_c[0] = sum_four(four_z)
+    yield from swap(net, at_step(two_c, 0), at_step(two_c, 1), at.other)
+    four_y[at.y] = two_c[0] + two_c[1]
     yield from spread(net, lambda p: four_y.at[p], at.y, at.dy[1:])
-    two_y[0] = sum_four(four_y)
-    yield from swap(net, at_step(two_y, 0), at_step(two_y, 1), at.other)
-    four_z[at.z] = two_y[0] + two_y[1]
-    yield from spread(net, lambda p: four_z.at[p], at.z, at.dz[1:])
-    two_z[0] = sum_four(four_z)
-    yield from swap(net, at_step(two_z, 0), at_step(two_z, 1), at.dx[2])
-    total[...] = two_z[0] + two_z[1]
+    total[...] = sum_four(four_y)
 
 
 def exact_dot(left, right):
@@ -412,6 +414,7 @@
     for copy in own:
         copy.wait()
 
+    step(bring_a, bring_b)
     s["times"][0:32] = jnp.zeros((32, RANK), F32)
     s["times"][32:64] = c_full[at.t].astype(F32)
     prefix[0] = jnp.zeros((EDGE, RANK), F32)
@@ -421,11 +424,10 @@
     make_plan(s["plan"], s["coords"], count[0])
     tell = pltpu.make_async_copy(s["plan"], plan, local.at[4 + LOADS])
     tell.start()
-    step(bring_a, bring_b)
+    step(bring_a)
     tell.wait()
     for copy in loads:
         copy.wait()
-    step(bring_a)
     drive(bring_b, bring_a, bring_c)
 
     s["gram"][...] = gram(b_full.reshape(16 * EDGE, RANK))
@@ -449,16 +451,16 @@
     pick = (snaps == iota((32, LANES), 0) + 32).astype(F32).astype(BF16)
     s["part_c"][...] = exact_dot(pick, s["dots"][...])
     part_c = reduce_time(
-        net, at, s["part_c"], s["cy4"], s["cy2"], s["cz4"], s["cz2"], s["total_c"]
+        net, at, s["part_c"], s["cx2"], s["cz4"], s["cc2"], s["cy4"], s["total_c"]
     )
     step(part_c)
     hooks = {
         1: lambda: step(share_a),
         2: lambda: step(share_b),
-        4: lambda: step(part_a, share_a),
+        3: lambda: step(part_a),
+        4: lambda: step(share_a),
         5: lambda: step(part_c),
-        7: lambda: step(part_c),
-        9: lambda: step(share_b, share_a),
+        9: lambda: step(share_b, share_a, part_c),
     }
     tile_pass(plan, 3, held, s["times"], a_flat, True, prefix, hooks)
 
@@ -485,16 +487,14 @@
     ]
     for _ in range(4):
         step(*part_b)
-    step(share_a, part_c)
+    step(share_a, part_c, part_a)
     whole_a = s["ga"][...].reshape(RANK, RANK)
     whole_b = s["gb"][...].reshape(RANK, RANK)
     whole_c = gram(c_full.reshape(64, RANK))
     s["near_a"][...] = exact_dot(a_full[at.y, at.core, at.t], whole_b * whole_c)
     s["near_b"][...] = exact_dot(b_full[at.z, at.x], whole_a * whole_c)
-    step(*part_b)
-    step(part_a)
-    step(*part_b)
-    step(*part_b)
+    for _ in range(3):
+        step(*part_b)
     step(part_c)
     grad_c[...] = exact_dot(c_full[at.t], whole_a * whole_b) - s["total_c"][...]
     step(*part_b)
@@ -536,14 +536,14 @@
         plan=pltpu.VMEM((8, LANES), jnp.int32), coords=pltpu.VMEM((3, 1, SLOTS), jnp.int32),
         chip=real(4, 2, EDGE), total_a=real(EDGE), total_b=real(EDGE), total_c=real(32),
         core_s=wire(4, 2, big), core_r=wire(4, 2, big),
-        y_s=wire(4, 2, big), y_r=wire(4, 2, big), x_s=wire(big), x_r=wire(big),
+        x_s=wire(4, big), x_r=wire(4, big), y_s=wire(4, big), y_r=wire(4, big),
         s10=half(4, 4, big), r10=half(4, 4, big), s20=half(4, big), r20=half(4, big),
         s11=half(4, 4, big), r11=half(4, 4, big), s21=half(4, big), r21=half(4, big),
         here0=pltpu.VMEM((EDGE, EDGE), F32), here1=pltpu.VMEM((EDGE, EDGE), F32),
         gram=real(RANK), gram_a=real(RANK), near_a=real(EDGE), near_b=real(EDGE),
         ga4=real(4, 16), ga2=real(2, 16), ga=real(4, 2, 2, 16),
         gb4=real(4, 16), gb2=real(2, 16), gb=real(4, 4, 16),
-        cy4=real(4, 32), cy2=real(2, 32), cz4=real(4, 32), cz2=real(2, 32),
+        cx2=real(2, 32), cz4=real(4, 32), cc2=real(2, 32), cy4=real(4, 32),
     )
     smem = pl.BlockSpec(memory_space=pltpu.SMEM)
     anywhere = pl.BlockSpec(memory_space=pl.ANY)

time: 64.2 us -> 60.4 us (0.941)
  Pallas kernels: 62.8 us -> 58.7 us
    pallas_call x1, Pallas kernels: 61.1 us -> 57 us  [on_device(): pl.pallas_call(gradient_kernel, out_shape=shapes, in_specs=[anywhere, sme...]
where the time goes in v5:
time: 60.4 us; the launch traced here: 60 us
  Pallas kernels  58.7 us (97%)
  between operations  1.28 us (2%)
    pallas_call x1, Pallas kernels, on_device(): pl.pallas_call(gradient_kernel, out_shape=shapes, in_specs=[anywhere, sme...  57 us
    pallas_call x1, Pallas kernels, on_device(): pl.pallas_call(hand_over, out_shape=shapes, in_specs=[anywhere] * 3, out_...  1.68 us

profile of v5, /device:TPU:0, one launch (start us, length us, event | category | flops | bytes accessed | tf_op | source)
XLA Modules:
  0.0 60.0 jit_solution(245182508294048424)
XLA Ops:
  1.3 57.0 %gradient.1 = (f32[1,128,256]{2,1,0:T(8,128)}, f32[1,128,256]{2,1,0:T(8,128)}, f32[32,256]{1,0:T(8,128)}) custom-call(s32[3,1,384]{2,1,0:T(1,128)} %bitcast.5, s32[1]{0:T(128)} %bitcast.3.count, bf16[384,128,128]{2,1,0:T(8,128)(2,1)} %bitcast.4, bf16[1,128,256]{2,1,0:T(8,128)(2,1)} %rows.1, bf16[1,128,256]{2,1,0:T(8,128)(2,1)} %cols.1, bf16[32,256]{1,0:T(8,128)(2,1)} %times.1), custom_call_target="tpu_custom_call" | custom-call | tf_op jit(solution)/shard_map/gradient/pallas_call | solution.py:557
  58.3 1.7 %hand_over.1 = (f32[1,128,256]{2,1,0:T(8,128)}, f32[1,128,256]{2,1,0:T(8,128)}, f32[32,256]{1,0:T(8,128)}) custom-call(f32[1,128,256]{2,1,0:T(8,128)} %get-tuple-element.6.in_a, f32[1,128,256]{2,1,0:T(8,128)} %get-tuple-element.7.in_b, f32[32,256]{1,0:T(8,128)} %get-tuple-element.8.in_c), custom_call_target="tpu_custom_call" | custom-call | tf_op jit(solution)/shard_map/hand_over/pallas_call | solution.py:574

commit v6 on v5

--- a/solution.py
+++ b/solution.py
@@ -70,12 +70,15 @@
         self.other = (row, self.y * 2 + self.far_core, self.t)
         self.pair = (row, col, self.far_t)
 
+        self.others = [self.other] + self.dz[1:] + self.dy[1:] + self.dx[1:]
+
     def greet(self):
         barrier = pltpu.get_barrier_semaphore()
-        others = [self.other] + self.dz[1:] + self.dy[1:] + self.dx[1:]
-        for device in others:
+        for device in self.others:
             pl.semaphore_signal(barrier, inc=1, device_id=device, device_id_type=MESH)
-        pl.semaphore_wait(barrier, len(others))
+
+    def await_all(self):
+        pl.semaphore_wait(pltpu.get_barrier_semaphore(), len(self.others))
 
 
 def step(run, *more):
@@ -104,12 +107,16 @@
     made.wait_recv()
 
 
+SPAN = 14.9999
+NEAREST = 12582912.0
+
+
 def encode(wire, value):
     rows = value.shape[0]
     top = jnp.max(jnp.abs(value), axis=0, keepdims=True)
     power = jnp.ceil(jnp.log2(jnp.maximum(top, 1e-30)))
-    coded = jnp.clip(value * jnp.exp2(15.0 - power), -32767.0, 32767.0)
-    wire[0:rows] = jnp.round(coded).astype(jnp.int32).astype(I16)
+    coded = value * jnp.exp2(SPAN - power)
+    wire[0:rows] = ((coded + NEAREST) - NEAREST).astype(jnp.int32).astype(I16)
     power = jnp.broadcast_to(power, (PAD, value.shape[1]))
     wire[rows : rows + PAD] = power.astype(jnp.int32).astype(I16)
 
@@ -117,7 +124,7 @@
 def decode(wire):
     rows = wire.shape[0] - PAD
     power = wire[rows : rows + PAD].astype(jnp.int32).astype(F32)[0:1]
-    return wire[0:rows].astype(jnp.int32).astype(F32) * jnp.exp2(power - 15.0)
+    return wire[0:rows].astype(jnp.int32).astype(F32) * jnp.exp2(power - SPAN)
 
 
 SLOTS = 384
@@ -268,60 +275,76 @@
     for k in order:
         for h in range(2):
             encode(s["core_s"].at[k, h], block(at.ys[k], at.far_core, h))
+    for k in order:
         made[k] = net.copy(at_step(s["core_s"], k), at_step(s["core_r"], k), at.other)
     for k in order:
         for h in range(2):
             chip[k, h] = block(at.ys[k], at.core, h)
     yield 1
-    paired = {}
+    sent = {}
     for k in order:
         made[k].wait_recv()
+    for k in order:
         for h in range(2):
-            chip[k, h] += decode(s["core_r"].at[k, h])
-        encode(s["x_s"].at[k], chip[k, at.far_t])
-        paired[k] = net.copy(at_step(s["x_s"], k), at_step(s["x_r"], k), at.pair)
-    yield 1
-    sent = {}
-    for k in order:
-        paired[k].wait_recv()
-        value = chip[k, at.t] + decode(s["x_r"].at[k])
-        if k:
-            encode(s["y_s"].at[k], value)
-            sent[k] = net.copy(at_step(s["y_s"], k), at_step(s["y_r"], k), at.dy[k])
-        else:
-            total[...] = value
+            value = chip[k, h] + decode(s["core_r"].at[k, h])
+            if k:
+                encode(s["y_s"].at[k, h], value)
+            else:
+                chip[0, h] = value
+    for k in (2, 1, 3):
+        sent[k] = net.copy(at_step(s["y_s"], k), at_step(s["y_r"], k), at.dy[k])
     yield 1
     for k in (1, 3, 2):
         sent[k].wait_recv()
-        total[...] += decode(s["y_r"].at[k])
-
-
-def reduce_cols(net, block, first, second, here, total, s1, r1, s2, r2):
+    for h in range(2):
+        value = chip[0, h]
+        for k in (1, 3, 2):
+            value = value + decode(s["y_r"].at[k, h])
+        chip[0, h] = value
+    encode(s["x_s"], chip[0, at.far_t])
+    yield from swap(net, s["x_s"], s["x_r"], at.pair)
+    total[...] = chip[0, at.t] + decode(s["x_r"])
+
+
+def reduce_cols(net, at, block, here, total, s):
     order = (2, 1, 3, 0)
-    made = {}
+    ways = ((at.dx, at.dz), (at.dz, at.dx))
+    part = (lambda k, j: block(k, j, 0), lambda k, j: block(j, k, 1))
+    s1, r1 = (s["s10"], s["s11"]), (s["r10"], s["r11"])
+    s2, r2 = (s["s20"], s["s21"]), (s["r20"], s["r21"])
+    made, sent = {}, {}
     for k in order:
         for j in (2, 1, 3):
-            encode(s1.at[k, j], block(k, j))
-            made[k, j] = net.copy(s1.at[k, j], r1.at[k, j], first[j])
+            for h in range(2):
+                encode(s1[h].at[k, j], part[h](k, j))
+        for j in (2, 1, 3):
+            for h in range(2):
+                made[h, k, j] = net.copy(s1[h].at[k, j], r1[h].at[k, j], ways[h][0][j])
         yield 1
-    sent = {}
     for k in order:
         for j in (1, 3, 2):
-            made[k, j].wait_recv()
-        value = block(k, 0)
-        for j in (1, 3, 2):
-            value = value + decode(r1.at[k, j])
-        if k:
-            encode(s2.at[k], value)
-            sent[k] = net.copy(s2.at[k], r2.at[k], second[k])
-        else:
-            here[...] = value
+            for h in range(2):
+                made[h, k, j].wait_recv()
+        for h in range(2):
+            value = part[h](k, 0)
+            for j in (1, 3, 2):
+                value = value + decode(r1[h].at[k, j])
+            if k:
+                encode(s2[h].at[k], value)
+            else:
+                here[h] = value
+        for h in range(2):
+            if k:
+                sent[h, k] = net.copy(s2[h].at[k], r2[h].at[k], ways[h][1][k])
         yield 1
-    value = here[...]
     for k in (2, 1, 3):
-        sent[k].wait_recv()
-        value = value + decode(r2.at[k])
-    total(value)
+        for h in range(2):
+            sent[h, k].wait_recv()
+    for h in range(2):
+        value = here[h]
+        for k in (2, 1, 3):
+            value = value + decode(r2[h].at[k])
+        total[:, 128 * h : 128 * h + 128] = value
 
 
 def sum_four(ref):
@@ -335,8 +358,9 @@
     two[0] = sum_four(four)
     yield from swap(net, at_step(two, 0), at_step(two, 1), at.dx[2])
     full[at.y, at.core, at.t] = two[0] + two[1]
-    yield from swap(net, lambda: full.at[at.y, at.core, at.t], lambda: full.at[at.y, at.core, at.t], at.pair)
-    yield from spread(net, lambda p: full.at[p, at.core], at.y, at.dy[1:])
+    yield from spread(net, lambda p: full.at[p, at.core, at.t], at.y, at.dy[1:])
+    column = lambda: full.at[:, at.core, at.t]
+    yield from swap(net, column, column, at.pair)
     yield from swap(net, lambda: full.at[:, at.core], lambda: full.at[:, at.core], at.other)
 
 
@@ -347,8 +371,8 @@
     two[0] = sum_four(four)
     yield from swap(net, at_step(two, 0), at_step(two, 1), at.other)
     full[at.z, at.x] = two[0] + two[1]
-    yield from spread(net, lambda p: full.at[p, at.x], at.z, at.dz[1:])
-    yield from spread(net, lambda p: full.at[:, p], at.x, at.dx[1:])
+    yield from spread(net, lambda p: full.at[at.z, p], at.x, at.dx[1:])
+    yield from spread(net, lambda p: full.at[p], at.z, at.dz[1:])
 
 
 def reduce_time(net, at, part, two_x, four_z, two_c, four_y, total):
@@ -384,6 +408,7 @@
     coords, count, values, rows, cols, times, grad_a, grad_b, grad_c, s, plan, send, recv, local
 ):
     at = Place()
+    at.greet()
     net = Net(send, recv)
     a_full, b_full, c_full = s["a"], s["b"], s["c"]
     a_flat = a_full.reshape(16, EDGE, RANK)
@@ -404,7 +429,7 @@
         )
         for i in range(LOADS)
     ]
-    at.greet()
+    at.await_all()
     bring_b = gather_cols(net, at, b_full, cols.at[0])
     bring_a = gather_rows(net, at, a_full, rows.at[0])
     bring_c = swap(net, times, c_full.at[at.t], at.pair)
@@ -428,11 +453,11 @@
     tell.wait()
     for copy in loads:
         copy.wait()
-    drive(bring_b, bring_a, bring_c)
-
+    drive(bring_b, bring_c)
     s["gram"][...] = gram(b_full.reshape(16 * EDGE, RANK))
     share_b = gram_cols(net, at, s["gram"], s["gb4"], s["gb2"], s["gb"])
     step(share_b)
+    drive(bring_a)
     s["gram_a"][...] = gram(a_full.reshape(16 * EDGE, RANK))
     share_a = gram_rows(net, at, s["gram_a"], s["ga4"], s["ga2"], s["ga"])
     step(share_a)
@@ -458,51 +483,46 @@
         1: lambda: step(share_a),
         2: lambda: step(share_b),
         3: lambda: step(part_a),
-        4: lambda: step(share_a),
         5: lambda: step(part_c),
+        6: lambda: step(share_a),
         9: lambda: step(share_b, share_a, part_c),
     }
     tile_pass(plan, 3, held, s["times"], a_flat, True, prefix, hooks)
 
     def col_block(z, x, h):
-        i = z * 4 + x
+        i = at.zs[z] * 4 + at.xs[x]
         lanes = slice(128 * h, 128 * h + 128)
         return prefix[plan[5, i], :, lanes] - prefix[plan[4, i], :, lanes]
 
-    def put(h):
-        def total(value):
-            s["total_b"][:, 128 * h : 128 * h + 128] = value
-
-        return total
-
-    part_b = [
-        reduce_cols(
-            net, lambda k, j: col_block(at.zs[k], at.xs[j], 0),
-            at.dx, at.dz, s["here0"], put(0), s["s10"], s["r10"], s["s20"], s["r20"],
-        ),
-        reduce_cols(
-            net, lambda k, j: col_block(at.zs[j], at.xs[k], 1),
-            at.dz, at.dx, s["here1"], put(1), s["s11"], s["r11"], s["s21"], s["r21"],
-        ),
-    ]
+    part_b = reduce_cols(net, at, col_block, s["here"], s["total_b"], s)
     for _ in range(4):
-        step(*part_b)
-    step(share_a, part_c, part_a)
+        step(part_b)
+    step(share_a, part_c)
     whole_a = s["ga"][...].reshape(RANK, RANK)
     whole_b = s["gb"][...].reshape(RANK, RANK)
     whole_c = gram(c_full.reshape(64, RANK))
     s["near_a"][...] = exact_dot(a_full[at.y, at.core, at.t], whole_b * whole_c)
     s["near_b"][...] = exact_dot(b_full[at.z, at.x], whole_a * whole_c)
-    for _ in range(3):
-        step(*part_b)
+    step(part_b)
+    step(part_a)
+    for _ in range(2):
+        step(part_b)
     step(part_c)
-    grad_c[...] = exact_dot(c_full[at.t], whole_a * whole_b) - s["total_c"][...]
-    step(*part_b)
+    s["out_c"][...] = exact_dot(c_full[at.t], whole_a * whole_b) - s["total_c"][...]
+    gone_c = pltpu.make_async_copy(s["out_c"], grad_c, local.at[0])
+    gone_c.start()
+    step(part_b)
     step(part_a)
-    grad_a[0] = s["near_a"][...] - s["total_a"][...]
-    drive(*part_b)
-    grad_b[0] = s["near_b"][...] - s["total_b"][...]
+    s["near_a"][...] = s["near_a"][...] - s["total_a"][...]
+    gone_a = pltpu.make_async_copy(s["near_a"], grad_a.at[0], local.at[1])
+    gone_a.start()
+    drive(part_b)
+    s["near_b"][...] = s["near_b"][...] - s["total_b"][...]
+    gone_b = pltpu.make_async_copy(s["near_b"], grad_b.at[0], local.at[2])
+    gone_b.start()
     net.close()
+    for copy in (gone_a, gone_b, gone_c):
+        copy.wait()
 
 
 def hand_over(in_a, in_b, in_c, out_a, out_b, out_c, held_a, held_b, held_c, sems):
@@ -536,18 +556,17 @@
         plan=pltpu.VMEM((8, LANES), jnp.int32), coords=pltpu.VMEM((3, 1, SLOTS), jnp.int32),
         chip=real(4, 2, EDGE), total_a=real(EDGE), total_b=real(EDGE), total_c=real(32),
         core_s=wire(4, 2, big), core_r=wire(4, 2, big),
-        x_s=wire(4, big), x_r=wire(4, big), y_s=wire(4, big), y_r=wire(4, big),
+        y_s=wire(4, 2, big), y_r=wire(4, 2, big), x_s=wire(big), x_r=wire(big),
         s10=half(4, 4, big), r10=half(4, 4, big), s20=half(4, big), r20=half(4, big),
         s11=half(4, 4, big), r11=half(4, 4, big), s21=half(4, big), r21=half(4, big),
-        here0=pltpu.VMEM((EDGE, EDGE), F32), here1=pltpu.VMEM((EDGE, EDGE), F32),
-        gram=real(RANK), gram_a=real(RANK), near_a=real(EDGE), near_b=real(EDGE),
+        here=pltpu.VMEM((2, EDGE, EDGE), F32),
+        gram=real(RANK), gram_a=real(RANK), near_a=real(EDGE), near_b=real(EDGE), out_c=real(32),
         ga4=real(4, 16), ga2=real(2, 16), ga=real(4, 2, 2, 16),
         gb4=real(4, 16), gb2=real(2, 16), gb=real(4, 4, 16),
         cx2=real(2, 32), cz4=real(4, 32), cc2=real(2, 32), cy4=real(4, 32),
     )
     smem = pl.BlockSpec(memory_space=pltpu.SMEM)
     anywhere = pl.BlockSpec(memory_space=pl.ANY)
-    whole = pl.BlockSpec(memory_space=pltpu.VMEM)
     shapes = (
         jax.ShapeDtypeStruct((1, EDGE, RANK), F32),
         jax.ShapeDtypeStruct((1, EDGE, RANK), F32),
@@ -558,7 +577,7 @@
         gradient_kernel,
         out_shape=shapes,
         in_specs=[anywhere, smem] + [anywhere] * 4,
-        out_specs=(whole,) * 3,
+        out_specs=(anywhere,) * 3,
         scratch_shapes=[
             scratch,
             pltpu.SMEM((8, LANES), jnp.int32),

time: 60.4 us -> 59.8 us (0.990)
  no operation moved by 1% of the time
where the time goes in v6:
time: 59.8 us; the launch traced here: 59.6 us
  Pallas kernels  58.4 us (98%)
  between operations  1.28 us (2%)
    pallas_call x1, Pallas kernels, on_device(): pl.pallas_call(gradient_kernel, out_shape=shapes, in_specs=[anywhere, sme...  56.7 us
    pallas_call x1, Pallas kernels, on_device(): pl.pallas_call(hand_over, out_shape=shapes, in_specs=[anywhere] * 3, out_...  1.68 us

profile of v6, /device:TPU:0, one launch (start us, length us, event | category | flops | bytes accessed | tf_op | source)
XLA Modules:
  0.0 59.6 jit_solution(5933887877425784665)
XLA Ops:
  1.3 56.7 %gradient.1 = (f32[1,128,256]{2,1,0:T(8,128)}, f32[1,128,256]{2,1,0:T(8,128)}, f32[32,256]{1,0:T(8,128)}) custom-call(s32[3,1,384]{2,1,0:T(1,128)} %bitcast.5, s32[1]{0:T(128)} %bitcast.3.count, bf16[384,128,128]{2,1,0:T(8,128)(2,1)} %bitcast.4, bf16[1,128,256]{2,1,0:T(8,128)(2,1)} %rows.1, bf16[1,128,256]{2,1,0:T(8,128)(2,1)} %cols.1, bf16[32,256]{1,0:T(8,128)(2,1)} %times.1), custom_call_target="tpu_custom_call" | custom-call | tf_op jit(solution)/shard_map/gradient/pallas_call | solution.py:576
  58.0 1.7 %hand_over.1 = (f32[1,128,256]{2,1,0:T(8,128)}, f32[1,128,256]{2,1,0:T(8,128)}, f32[32,256]{1,0:T(8,128)}) custom-call(f32[1,128,256]{2,1,0:T(8,128)} %get-tuple-element.6.in_a, f32[1,128,256]{2,1,0:T(8,128)} %get-tuple-element.7.in_b, f32[32,256]{1,0:T(8,128)} %get-tuple-element.8.in_c), custom_call_target="tpu_custom_call" | custom-call | tf_op jit(solution)/shard_map/hand_over/pallas_call | solution.py:593

commit v7 on v6

--- a/solution.py
+++ b/solution.py
@@ -132,7 +132,7 @@
 PADDED = SLOTS + 16 * (ROUND - 1)
 ROUNDS = PADDED // ROUND
 LANES = 512
-UNROLL = 40
+UNROLL = 80
 LOADS = 12
 
 
@@ -458,10 +458,13 @@
     share_b = gram_cols(net, at, s["gram"], s["gb4"], s["gb2"], s["gb"])
     step(share_b)
     drive(bring_a)
-    s["gram_a"][...] = gram(a_full.reshape(16 * EDGE, RANK))
     share_a = gram_rows(net, at, s["gram_a"], s["ga4"], s["ga2"], s["ga"])
-    step(share_a)
-    hooks = {5: lambda: step(share_b, share_a), 7: lambda: step(share_b)}
+
+    def start_a():
+        s["gram_a"][...] = gram(a_full.reshape(16 * EDGE, RANK))
+        step(share_a)
+
+    hooks = {0: start_a, 3: lambda: step(share_b, share_a), 4: lambda: step(share_b)}
     tile_pass(
         plan, 0, held, s["times"], b_flat, False, prefix, hooks, a_flat, s["dots"]
     )
@@ -480,12 +483,9 @@
     )
     step(part_c)
     hooks = {
-        1: lambda: step(share_a),
-        2: lambda: step(share_b),
-        3: lambda: step(part_a),
-        5: lambda: step(part_c),
-        6: lambda: step(share_a),
-        9: lambda: step(share_b, share_a, part_c),
+        1: lambda: step(share_a, share_b),
+        2: lambda: step(part_a, part_c),
+        3: lambda: step(share_a),
     }
     tile_pass(plan, 3, held, s["times"], a_flat, True, prefix, hooks)
 
@@ -495,6 +495,7 @@
         return prefix[plan[5, i], :, lanes] - prefix[plan[4, i], :, lanes]
 
     part_b = reduce_cols(net, at, col_block, s["here"], s["total_b"], s)
+    step(share_b, share_a, part_c)
     for _ in range(4):
         step(part_b)
     step(share_a, part_c)

time: 59.8 us -> 57.6 us (0.963)
  Pallas kernels: 58.4 us -> 56.2 us
    pallas_call x1, Pallas kernels: 56.7 us -> 54.5 us  [on_device(): pl.pallas_call(gradient_kernel, out_shape=shapes, in_specs=[anywhere, sme...]
where the time goes in v7:
time: 57.6 us; the launch traced here: 57.5 us
  Pallas kernels  56.2 us (98%)
  between operations  1.28 us (2%)
    pallas_call x1, Pallas kernels, on_device(): pl.pallas_call(gradient_kernel, out_shape=shapes, in_specs=[anywhere, sme...  54.5 us
    pallas_call x1, Pallas kernels, on_device(): pl.pallas_call(hand_over, out_shape=shapes, in_specs=[anywhere] * 3, out_...  1.68 us

profile of v7, /device:TPU:0, one launch (start us, length us, event | category | flops | bytes accessed | tf_op | source)
XLA Modules:
  0.0 57.5 jit_solution(670007977866497895)
XLA Ops:
  1.3 54.5 %gradient.1 = (f32[1,128,256]{2,1,0:T(8,128)}, f32[1,128,256]{2,1,0:T(8,128)}, f32[32,256]{1,0:T(8,128)}) custom-call(s32[3,1,384]{2,1,0:T(1,128)} %bitcast.5, s32[1]{0:T(128)} %bitcast.3.count, bf16[384,128,128]{2,1,0:T(8,128)(2,1)} %bitcast.4, bf16[1,128,256]{2,1,0:T(8,128)(2,1)} %rows.1, bf16[1,128,256]{2,1,0:T(8,128)(2,1)} %cols.1, bf16[32,256]{1,0:T(8,128)(2,1)} %times.1), custom_call_target="tpu_custom_call" | custom-call | tf_op jit(solution)/shard_map/gradient/pallas_call | solution.py:577
  55.8 1.7 %hand_over.1 = (f32[1,128,256]{2,1,0:T(8,128)}, f32[1,128,256]{2,1,0:T(8,128)}, f32[32,256]{1,0:T(8,128)}) custom-call(f32[1,128,256]{2,1,0:T(8,128)} %get-tuple-element.6.in_a, f32[1,128,256]{2,1,0:T(8,128)} %get-tuple-element.7.in_b, f32[32,256]{1,0:T(8,128)} %get-tuple-element.8.in_c), custom_call_target="tpu_custom_call" | custom-call | tf_op jit(solution)/shard_map/hand_over/pallas_call | solution.py:594
